TPU v7x, 512 devices: a whole 4x4x16 slice. The times are simulated.
512 devices in a mesh: dp: 64 (over z, x), tensor: 8 (over y, core).
Axes of the slice: x: 4, y: 4, z: 16, core: 2. Of those that a mesh axis runs over, the one named last changes fastest.
Arguments:
- grads: float32 [64, 8, 524288], P('dp', 'tensor'), may hold values from -16 to 16
- piece_lengths: int32 [40], replicated, may hold values from 1 to 65536
- split_flags: int32 [40], replicated, may hold values from 0 to 1
- master_params: float32 [8, 524288], P('tensor', 'dp'), may hold values from -16 to 16
- exp_avg: float32 [8, 524288], P('tensor', 'dp'), may hold values from -0.3 to 0.3
- exp_avg_sq: float32 [8, 524288], P('tensor', 'dp'), may hold values from 0.001 to 0.1
Outputs:
- new_master: float32 [8, 524288], P('tensor', 'dp')
- new_avg: float32 [8, 524288], P('tensor', 'dp')
- new_avg_sq: float32 [8, 524288], P('tensor', 'dp')
- model_params: bfloat16 [8, 524288], P('tensor')
All inputs are finite; a program needn't handle non-finite values.
Results may differ from a plain program's by a relative error of at most 0.0004.
Values may be sent and summed in bfloat16 or wider, within the bound.
A program may use at most 64 MiB of HBM per device.

v0:
```python
import jax
import jax.numpy as jnp
from jax import lax
from jax.sharding import PartitionSpec as P


def moments(grad, weights, first, second):
    new_first = 0.9 * first + 0.1 * grad
    new_second = 0.95 * second + 0.05 * grad * grad
    update = new_first / (jnp.sqrt(new_second) + 1e-08) + 0.1 * weights
    return (new_first, new_second, update)


def local(grads, piece_lengths, split_flags, master_params, exp_avg, exp_avg_sq):
    replicas = lax.axis_size("dp")
    width = master_params.shape[1]
    terms = grads[0, 0].reshape(replicas, width)
    weights = master_params[0]
    first = exp_avg[0]
    second = exp_avg_sq[0]
    grad = lax.psum_scatter(terms, "dp", scatter_dimension=0, tiled=True)[0] / replicas
    new_first, new_second, update = moments(grad, weights, first, second)
    ends = jnp.cumsum(piece_lengths)
    starts = ends - piece_lengths
    position = lax.axis_index("dp") * width + jnp.arange(width, dtype=jnp.int32)
    inside = (position[:, None] >= starts[None, :]) & (position[:, None] < ends[None, :])
    member = inside.astype(jnp.float32)
    squares = jnp.stack([weights * weights, update * update])
    partials = jnp.dot(
        squares, member, precision=lax.Precision.HIGHEST, preferred_element_type=jnp.float32
    )
    split = (split_flags == 1)[None, :]
    data_sum = lax.psum(partials, "dp")
    tensor_sum = lax.psum(data_sum, "tensor")
    effective = jnp.where(split, tensor_sum, data_sum)
    trust = jnp.sqrt(effective[0]) / jnp.maximum(jnp.sqrt(effective[1]), 1.0)
    trust_at = jnp.dot(
        member, trust, precision=lax.Precision.HIGHEST, preferred_element_type=jnp.float32
    )
    new_weights = weights - 0.05 * trust_at * update
    gathered = lax.all_gather(new_weights.astype(jnp.bfloat16)[None, :], "dp", axis=1, tiled=True)
    return (new_weights[None, :], new_first[None, :], new_second[None, :], gathered)


def solution(mesh):
    return jax.shard_map(
        local,
        mesh=mesh,
        in_specs=(
            P("dp", "tensor", None),
            P(),
            P(),
            P("tensor", "dp"),
            P("tensor", "dp"),
            P("tensor", "dp"),
        ),
        out_specs=(P("tensor", "dp"), P("tensor", "dp"), P("tensor", "dp"), P("tensor", None)),
        check_vma=False,
    )
```

profile of v0, /device:TPU:6, one launch (start us, length us, event | category | flops | bytes accessed | tf_op | source)
XLA Modules:
  0.0 608.9 jit_solution(15816515173466458874)
XLA Ops:
  7.2 0.0 all-reduce.3.cloned.1.call-start
  7.2 0.5 broadcast.53
  7.7 19.0 %reduce.4 = f32[524288]{0:T(1024)S(1)} reduce(f32[1,1,524288]{2,1,0:T(1,128)} %param.6, f32[]{:T(128)} %broadcast.53), dimensions={0,1}, to_apply=%param.6.reduce_sub_computation.3 | reduce | bytes 4194308 | tf_op args[0]
  26.8 1.5 reshape_squeeze.3
  28.3 0.0 copy-start.3
  28.3 0.0 copy-start.4
  28.3 0.0 copy-start
  28.3 0.0 copy-start.1
  28.3 0.0 copy-start.2
  28.3 0.0 all-reduce.3.cloned.1.call-update
  28.3 0.0 all-gather.3.cloned.1.call-start
  28.4 0.5 copy-done.3
  29.0 0.1 copy.13
  29.0 0.1 reduce-window.8
  29.1 0.1 reduce
  29.2 1.3 dynamic-slice
  30.5 0.0 copy-done.4
  30.5 279.0 %all-reduce.3.cloned.1.call-done = f32[64,8192]{1,0:T(8,128)} async-done(((f32[64,8192]{1,0:T(8,128)}), f32[64,8192]{1,0:T(8,128)}) %all-reduce.3.cloned.1.call-update) | async-done | bytes 2097168
  309.6 0.0 copy-done
  309.6 0.0 copy-done.1
  309.6 0.0 copy-done.2
  309.6 2.4 add_multiply_fusion
  312.0 0.8 fusion.1
  312.9 136.1 %psum.14 = f32[2,40]{1,0:T(2,128)S(1)} all-reduce(f32[2,40]{1,0:T(2,128)S(1)} %fusion.1), channel_id=1, replica_groups=mesh['dp'=64,'tensor'=8] {'dp'}, use_global_device_ids=true, to_apply=%region_2.3 | all-reduce | flops 80 | bytes 640 | tf_op jit(solution)/shard_map/psum | solution.py:33
  448.9 12.4 %psum.15 = f32[2,40]{1,0:T(2,128)S(1)} all-reduce(f32[2,40]{1,0:T(2,128)S(1)} %psum.14), channel_id=1, replica_groups=mesh['dp'=64,'tensor'=8] {'tensor'}, use_global_device_ids=true, to_apply=%region_3.4 | all-reduce | flops 80 | bytes 640 | tf_op jit(solution)/shard_map/psum | solution.py:34
  461.3 0.6 fusion
  462.0 0.6 fusion.14
  462.6 0.0 all-gather.3.cloned.1.call-update
  462.6 135.4 %all-gather.3.cloned.1.call-done = bf16[524288]{0:T(1024)(128)(2,1)} async-done(((bf16[8192]{0:T(1024)(128)(2,1)}), bf16[524288]{0:T(1024)(128)(2,1)}) %all-gather.3.cloned.1.call-update) | async-done | bytes 1048592 | tf_op jit(solution)/shard_map/all_gather | solution.py:41
  598.0 4.0 reshape.61
  (4 shorter events, 0.0 us)
Async XLA Ops:
  7.2 302.4 %all-reduce.3.cloned.1.call-start = ((), (), s32[]{:S(2)}) async-start(), calls=%async_computation.1 | async-start | bytes 4194304
  28.3 0.7 copy-start.3
  28.3 2.2 copy-start.4
  28.3 281.3 %copy-start = (f32[1,8192]{1,0:T(1,128)S(1)}, f32[1,8192]{1,0:T(1,128)}, u32[]{:S(2)}) copy-start(f32[1,8192]{1,0:T(1,128)} %param.9) | copy-start | bytes 98308
  28.3 281.3 %copy-start.1 = (f32[1,8192]{1,0:T(1,128)S(1)}, f32[1,8192]{1,0:T(1,128)}, u32[]{:S(2)}) copy-start(f32[1,8192]{1,0:T(1,128)} %param.11) | copy-start | bytes 98308
  28.3 281.3 %copy-start.2 = (f32[1,8192]{1,0:T(1,128)S(1)}, f32[1,8192]{1,0:T(1,128)}, u32[]{:S(2)}) copy-start(f32[1,8192]{1,0:T(1,128)} %param.10) | copy-start | bytes 98308
  28.3 569.7 %all-gather.3.cloned.1.call-start = ((), (), s32[]{:S(2)}) async-start(), calls=%async_computation | async-start | bytes 1064960 | tf_op jit(solution)/shard_map/all_gather | solution.py:41
Sparse Core Ops, SparseCore 0:
  28.5 281.0 all-reduce.2
  462.8 135.2 all-gather.2
where the time goes:
time: 610 us; the launch traced here: 609 us
  waiting for transfers between devices  414 us (68%)
  blocking collectives  148 us (24%)
  other arithmetic  22.3 us (4%)
  between operations  14.1 us (2%)
  local copies, waits for them, and re-layouts  8.01 us (1%)
    unnamed x3, waiting for transfers between devices  279 us
    psum x1, blocking collectives, local(): data_sum = lax.psum(partials, 'dp')  136 us
    all_gather x1, waiting for transfers between devices, local(): lax.all_gather(new_weights.astype(jnp.bfloat16)[None, :], 'dp', axis=1, t...  135 us
    unnamed x1, other arithmetic  19 us
    psum x1, blocking collectives, local(): tensor_sum = lax.psum(data_sum, 'tensor')  12.4 us
  transfers between devices with their start and end apart: 2, of which 2 were waited for; matrix products, arithmetic and copies ran while one was open for 0% of the time, Pallas kernels for 0%

commit v1 on v0

v1 whole, which is shorter than its diff:
```python
import jax
import jax.numpy as jnp
from jax import lax
from jax.experimental import pallas as pl
from jax.experimental.pallas import tpu as pltpu
from jax.sharding import PartitionSpec as P

MESH = pl.DeviceIdType.MESH
NZ, NX, NT = 16, 4, 8
GROUP = 4
ROWS = 64
WORDS = 32
NP = 40
XROWS = GROUP * WORDS + 8
ORDER = (2, 1, 3, 0)


def encode(block, unit):
    top = jnp.max(jnp.abs(block), axis=0, keepdims=True)
    scale = (top * unit).astype(jnp.int32) + 1
    inverse = (32767.0 * unit) / scale.astype(jnp.float32)
    codes = jnp.round(block * inverse).astype(jnp.int32)
    return (codes[:WORDS] << 16) + codes[WORDS:], scale


def decode(words, scale, unit):
    step = scale.astype(jnp.float32) * (1.0 / (32767.0 * unit))
    high = ((words + 32768) >> 16).astype(jnp.float32) * step
    low = ((words << 16) >> 16).astype(jnp.float32) * step
    return high, low


UNIT_X = float(2**26)
UNIT_Z = float(2**24)


def piece_sums(values, position, starts):
    rows = []
    for k in range(NP):
        inside = (position >= starts[k]) & (position < starts[k + 1])
        rows.append(jnp.sum(jnp.where(inside, values, 0.0), axis=0, keepdims=True))
    table = jnp.concatenate(rows, axis=0)
    totals = jnp.sum(table, axis=1, keepdims=True)
    piece = lax.broadcasted_iota(jnp.int32, (NP, 128), 0)
    lane = lax.broadcasted_iota(jnp.int32, (NP, 128), 1)
    return jnp.sum(jnp.where(piece == lane, totals, 0.0), axis=0, keepdims=True)


def kernel(
    lengths, flags, grads, master, avg, avg_sq,
    out_master, out_avg, out_avg_sq, out_model,
    held, coded, x_in, z_out, z_in, total, state, stat_z, stat_p, weights,
    load_sem, state_sem, xs_sem, xr_sem, zs_sem, zr_sem, ns_sem, nr_sem, ps_sem, pr_sem,
    gs_sem, gr_sem, fs_sem, fr_sem,
):
    dp = lax.axis_index("dp")
    t = lax.axis_index("tensor")
    z, x = dp // NX, dp % NX
    home = z // GROUP

    def group_of(k):
        return (home + k) % GROUP

    def at(zz, xx, tt):
        return (zz * NX + xx, tt)

    def load(k):
        rows = pl.ds(pl.multiple_of(group_of(k) * 1024, 1024), 1024)
        return pltpu.make_async_copy(grads.at[rows], held.at[rows], load_sem.at[k])

    for k in ORDER:
        load(k).start()
    state_copies = [
        pltpu.make_async_copy(ref, state.at[i], state_sem.at[i])
        for i, ref in enumerate((master, avg, avg_sq))
    ]
    for copy in state_copies:
        copy.start()

    barrier = pltpu.get_barrier_semaphore()

    def hail_z(o, c):
        pl.semaphore_signal(barrier, 1, device_id=at((z + o) % NZ, x, t), device_id_type=MESH)
        return c

    lax.fori_loop(1, NZ, hail_z, 0)

    def plane(o):
        me = x * NT + t
        other = (me + o) % (NX * NT)
        return other // NT, other % NT

    def hail_p(o, c):
        xx, tt = plane(o)
        pl.semaphore_signal(barrier, 1, device_id=at(z, xx, tt), device_id_type=MESH)
        return c

    lax.fori_loop(1, NX * NT, hail_p, 0)

    def x_copy(k, o):
        a = group_of(k)
        xx = (x + o) % NX
        return pltpu.make_async_remote_copy(
            src_ref=coded.at[xx, a], dst_ref=x_in.at[x, a],
            send_sem=xs_sem.at[o, k], recv_sem=xr_sem.at[x, a],
            device_id=at(z, xx, t), device_id_type=MESH,
        )

    def x_arrival(k, o):
        a = group_of(k)
        xx = (x + o) % NX
        return pltpu.make_async_remote_copy(
            src_ref=coded.at[xx, a], dst_ref=x_in.at[xx, a],
            send_sem=xs_sem.at[o, k], recv_sem=xr_sem.at[xx, a],
            device_id=at(z, xx, t), device_id_type=MESH,
        )

    for n, k in enumerate(ORDER):
        a = group_of(k)
        load(k).wait()

        def code(o, c, a=a):
            xx = (x + o) % NX
            for j in range(GROUP):
                start = pl.multiple_of(((a * GROUP + j) * NX + xx) * ROWS, ROWS)
                words, scale = encode(held[pl.ds(start, ROWS), :], UNIT_X)
                coded[xx, a, j * WORDS : (j + 1) * WORDS, :] = words
                coded[xx, a, GROUP * WORDS + j : GROUP * WORDS + j + 1, :] = scale
            return c

        lax.fori_loop(1, NX, code, 0)
        if n == 0:
            pl.semaphore_wait(barrier, NZ - 1 + NX * NT - 1)
        for o in (2, 1, 3):
            x_copy(k, o).start()

    starts = [jnp.int32(0)]
    for k in range(NP):
        starts.append(starts[-1] + lengths[k])
    position = (
        dp * (ROWS * 128)
        + lax.broadcasted_iota(jnp.int32, (ROWS, 128), 0) * 128
        + lax.broadcasted_iota(jnp.int32, (ROWS, 128), 1)
    )
    for copy in state_copies:
        copy.wait()
    w = state[0]
    w_sums = piece_sums(w * w, position, starts)

    def z_copy(zz):
        return pltpu.make_async_remote_copy(
            src_ref=z_out.at[zz, pl.ds(0, WORDS + 1)], dst_ref=z_in.at[z, pl.ds(0, WORDS + 1)],
            send_sem=zs_sem.at[zz], recv_sem=zr_sem.at[z],
            device_id=at(zz, x, t), device_id_type=MESH,
        )

    def z_arrival(zz):
        return pltpu.make_async_remote_copy(
            src_ref=z_out.at[zz, pl.ds(0, WORDS + 1)], dst_ref=z_in.at[zz, pl.ds(0, WORDS + 1)],
            send_sem=zs_sem.at[zz], recv_sem=zr_sem.at[zz],
            device_id=at(zz, x, t), device_id_type=MESH,
        )

    def sum_over_x(a, j):
        start = pl.multiple_of(((a * GROUP + j) * NX + x) * ROWS, ROWS)
        high = held[pl.ds(start, WORDS), :]
        low = held[pl.ds(pl.multiple_of(start + WORDS, WORDS), WORDS), :]
        for o in range(1, NX):
            xx = (x + o) % NX
            rows = pl.ds(pl.multiple_of(j * WORDS, WORDS), WORDS)
            tile = x_in[xx, a, GROUP * WORDS :, :]
            picked = lax.broadcasted_iota(jnp.int32, (8, 128), 0) == j
            scale = jnp.sum(jnp.where(picked, tile, 0), axis=0, keepdims=True)
            h, l = decode(x_in[xx, a, rows, :], scale, UNIT_X)
            high, low = high + h, low + l
        return high, low

    for k in ORDER:
        a = group_of(k)
        for o in (1, 3, 2):
            x_arrival(k, o).wait_recv()

        def forward(i, c, a=a, k=k):
            j = (z + i) % GROUP
            high, low = sum_over_x(a, j)
            words, scale = encode(jnp.concatenate([high, low], axis=0), UNIT_Z)
            zz = a * GROUP + j
            z_out[zz, :WORDS, :] = words
            z_out[zz, WORDS : WORDS + 1, :] = scale
            z_copy(zz).start()
            return c

        lax.fori_loop(1 if k == 0 else 0, GROUP, forward, 0)
    high, low = sum_over_x(home, z % GROUP)
    total[:WORDS, :] = high
    total[WORDS:, :] = low

    def collect(o, c):
        zz = (z + o) % NZ
        z_arrival(zz).wait_recv()
        h, l = decode(z_in[zz, :WORDS, :], z_in[zz, WORDS : WORDS + 1, :], UNIT_Z)
        total[:WORDS, :] += h
        total[WORDS:, :] += l
        return c

    lax.fori_loop(1, NZ, collect, 0)

    grad = total[...] * (1.0 / (NZ * NX))
    new_avg = 0.9 * state[1] + 0.1 * grad
    new_avg_sq = 0.95 * state[2] + 0.05 * grad * grad
    out_avg[...] = new_avg
    out_avg_sq[...] = new_avg_sq
    update = new_avg / (jnp.sqrt(new_avg_sq) + 1e-08) + 0.1 * state[0]
    total[...] = update
    u_sums = piece_sums(update * update, position, starts)

    stat_z[z, 0:1, :] = w_sums
    stat_z[z, 1:2, :] = u_sums

    def n_copy(o):
        zz = (z + o) % NZ
        return pltpu.make_async_remote_copy(
            src_ref=stat_z.at[z, pl.ds(0, 2)], dst_ref=stat_z.at[z, pl.ds(0, 2)],
            send_sem=ns_sem.at[o], recv_sem=nr_sem.at[z],
            device_id=at(zz, x, t), device_id_type=MESH,
        )

    def n_arrival(o):
        zz = (z + o) % NZ
        return pltpu.make_async_remote_copy(
            src_ref=stat_z.at[z, pl.ds(0, 2)], dst_ref=stat_z.at[zz, pl.ds(0, 2)],
            send_sem=ns_sem.at[o], recv_sem=nr_sem.at[zz],
            device_id=at(zz, x, t), device_id_type=MESH,
        )

    for o in (8, 7, 9, 6, 10, 5, 11, 4, 12, 3, 13, 2, 14, 1, 15):
        n_copy(o).start()
    for o in range(1, NZ):
        n_arrival(o).wait_recv()
    sums = stat_z[0, 0:2, :]
    for zz in range(1, NZ):
        sums = sums + stat_z[zz, 0:2, :]
    me = x * NT + t
    stat_p[me, 0:2, :] = sums

    def p_copy(o):
        xx, tt = plane(o)
        return pltpu.make_async_remote_copy(
            src_ref=stat_p.at[me, pl.ds(0, 2)], dst_ref=stat_p.at[me, pl.ds(0, 2)],
            send_sem=ps_sem.at[o], recv_sem=pr_sem.at[me],
            device_id=at(z, xx, tt), device_id_type=MESH,
        )

    def p_arrival(o):
        xx, tt = plane(o)
        return pltpu.make_async_remote_copy(
            src_ref=stat_p.at[me, pl.ds(0, 2)], dst_ref=stat_p.at[xx * NT + tt, pl.ds(0, 2)],
            send_sem=ps_sem.at[o], recv_sem=pr_sem.at[xx * NT + tt],
            device_id=at(z, xx, tt), device_id_type=MESH,
        )

    def start_p(o, c):
        p_copy(o).start()
        return c

    def wait_p(o, c):
        p_arrival(o).wait_recv()
        return c

    lax.fori_loop(1, NX * NT, start_p, 0)
    lax.fori_loop(1, NX * NT, wait_p, 0)
    data_sum = stat_p[t, 0:2, :]
    for xx in range(1, NX):
        data_sum = data_sum + stat_p[xx * NT + t, 0:2, :]
    tensor_sum = stat_p[0, 0:2, :]
    for i in range(1, NX * NT):
        tensor_sum = tensor_sum + stat_p[i, 0:2, :]
    effective = jnp.where(flags[0:1, :] == 1, tensor_sum, data_sum)
    trust = jnp.sqrt(effective[0:1]) / jnp.maximum(jnp.sqrt(effective[1:2]), 1.0)
    trust_at = jnp.broadcast_to(trust[:, 0:1], (ROWS, 128))
    for k in range(1, NP):
        trust_at = jnp.where(position >= starts[k], trust[:, k : k + 1], trust_at)
    new_weights = state[0] - 0.05 * trust_at * total[...]
    out_master[...] = new_weights

    weights[z, x] = new_weights.astype(jnp.bfloat16)

    def g_copy(o):
        zz = (z + o) % NZ
        return pltpu.make_async_remote_copy(
            src_ref=weights.at[z, x], dst_ref=weights.at[z, x],
            send_sem=gs_sem.at[o], recv_sem=gr_sem.at[z],
            device_id=at(zz, x, t), device_id_type=MESH,
        )

    def g_arrival(zz):
        return pltpu.make_async_remote_copy(
            src_ref=weights.at[z, x], dst_ref=weights.at[zz, x],
            send_sem=gs_sem.at[1], recv_sem=gr_sem.at[zz],
            device_id=at(zz, x, t), device_id_type=MESH,
        )

    for o in (8, 7, 9, 6, 10, 5, 11, 4, 12, 3, 13, 2, 14, 1, 15):
        g_copy(o).start()

    def f_copy(k, o):
        a = group_of(k)
        xx = (x + o) % NX
        blocks = weights.at[pl.ds(a * GROUP, GROUP), x]
        return pltpu.make_async_remote_copy(
            src_ref=blocks, dst_ref=blocks,
            send_sem=fs_sem.at[o, k], recv_sem=fr_sem.at[x, a],
            device_id=at(z, xx, t), device_id_type=MESH,
        )

    def f_arrival(k, o):
        a = group_of(k)
        xx = (x + o) % NX
        blocks = weights.at[pl.ds(a * GROUP, GROUP), xx]
        return pltpu.make_async_remote_copy(
            src_ref=blocks, dst_ref=blocks,
            send_sem=fs_sem.at[o, k], recv_sem=fr_sem.at[xx, a],
            device_id=at(z, xx, t), device_id_type=MESH,
        )

    for k in (0, 1, 3, 2):
        for i in range(1 if k == 0 else 0, GROUP):
            g_arrival(group_of(k) * GROUP + (z + i) % GROUP).wait_recv()
        for o in (2, 1, 3):
            f_copy(k, o).start()
    for k in (0, 1, 3, 2):
        for o in (1, 3, 2):
            f_arrival(k, o).wait_recv()
        a = group_of(k)
        for j in range(GROUP):
            for xx in range(NX):
                start = pl.multiple_of(((a * GROUP + j) * NX + xx) * ROWS, ROWS)
                out_model[pl.ds(start, ROWS), :] = weights[a * GROUP + j, xx]

    for k in ORDER:
        for o in range(1, NX):
            x_copy(k, o).wait_send()
            f_copy(k, o).wait_send()
    for o in range(1, NZ):
        z_copy((z + o) % NZ).wait_send()
        n_copy(o).wait_send()
        g_copy(o).wait_send()

    def end_p(o, c):
        p_copy(o).wait_send()
        return c

    lax.fori_loop(1, NX * NT, end_p, 0)


def local(grads, piece_lengths, split_flags, master_params, exp_avg, exp_avg_sq):
    vmem = pl.BlockSpec(memory_space=pltpu.VMEM)
    anywhere = pl.BlockSpec(memory_space=pltpu.HBM)
    shard = jax.ShapeDtypeStruct((ROWS, 128), jnp.float32)
    dma = pltpu.SemaphoreType.DMA
    flags = jnp.pad(split_flags, (0, 128 - NP)).reshape(1, 128)
    new_master, new_avg, new_avg_sq, model = pl.pallas_call(
        kernel,
        name="lamb",
        out_shape=(shard, shard, shard, jax.ShapeDtypeStruct((NZ * NX * ROWS, 128), jnp.bfloat16)),
        in_specs=[pl.BlockSpec(memory_space=pltpu.SMEM), vmem, anywhere, anywhere, anywhere, anywhere],
        out_specs=(vmem, vmem, vmem, vmem),
        scratch_shapes=[
            pltpu.VMEM((NZ * NX * ROWS, 128), jnp.float32),
            pltpu.VMEM((NX, GROUP, XROWS, 128), jnp.int32),
            pltpu.VMEM((NX, GROUP, XROWS, 128), jnp.int32),
            pltpu.VMEM((NZ, WORDS + 8, 128), jnp.int32),
            pltpu.VMEM((NZ, WORDS + 8, 128), jnp.int32),
            pltpu.VMEM((ROWS, 128), jnp.float32),
            pltpu.VMEM((3, ROWS, 128), jnp.float32),
            pltpu.VMEM((NZ, 8, 128), jnp.float32),
            pltpu.VMEM((NX * NT, 8, 128), jnp.float32),
            pltpu.VMEM((NZ, NX, ROWS, 128), jnp.bfloat16),
            dma((4,)), dma((3,)),
            dma((NX, 4)), dma((NX, 4)),
            dma((NZ,)), dma((NZ,)),
            dma((NZ,)), dma((NZ,)),
            dma((NX * NT,)), dma((NX * NT,)),
            dma((NZ,)), dma((NZ,)),
            dma((NX, 4)), dma((NX, 4)),
        ],
        compiler_params=pltpu.CompilerParams(
            collective_id=0, has_side_effects=True, vmem_limit_bytes=24 * 2**20
        ),
    )(
        piece_lengths, flags, grads.reshape(NZ * NX * ROWS, 128), master_params.reshape(ROWS, 128),
        exp_avg.reshape(ROWS, 128), exp_avg_sq.reshape(ROWS, 128),
    )
    return (
        new_master.reshape(1, -1), new_avg.reshape(1, -1), new_avg_sq.reshape(1, -1), model.reshape(1, -1)
    )


def solution(mesh):
    return jax.shard_map(
        local,
        mesh=mesh,
        in_specs=(
            P("dp", "tensor", None),
            P(),
            P(),
            P("tensor", "dp"),
            P("tensor", "dp"),
            P("tensor", "dp"),
        ),
        out_specs=(P("tensor", "dp"), P("tensor", "dp"), P("tensor", "dp"), P("tensor", None)),
        check_vma=False,
    )
```

time: 610 us -> 107 us (0.18)
  the two profiles are of different devices: /device:TPU:6 before, /device:TPU:1 now
where the time goes in v1:
time: 107 us; the launch traced here: 106 us
  Pallas kernels  81.6 us (76%)
  local copies, waits for them, and re-layouts  24.1 us (23%)
    pallas_call x1, Pallas kernels, local(): pl.pallas_call(kernel, name='lamb', out_shape=(shard, shard, shard, jax.S...  81.6 us
    unnamed x14, local copies, waits for them, and re-layouts  23.4 us

profile of v1, /device:TPU:1, one launch (start us, length us, event | category | flops | bytes accessed | tf_op | source)
XLA Modules:
  0.0 106.3 jit_solution(411683352052173822)
XLA Ops:
  0.6 0.7 pad_bitcast_fusion.flags
  1.3 0.0 copy-start
  1.3 1.6 %copy-done = f32[1,1,524288]{2,1,0:T(1,128)S(1)} copy-done((f32[1,1,524288]{2,1,0:T(1,128)S(1)}, f32[1,1,524288]{2,1,0:T(1,128)}, u32[]{:S(2)}) %copy-start) | copy-done | bytes 2097176
  2.9 0.0 copy-start.1
  2.9 0.8 copy-done.1
  3.6 0.0 copy-start.2
  3.6 0.8 copy-done.2
  4.4 0.0 copy-start.3
  4.4 0.8 copy-done.3
  5.2 0.0 copy-start.4
  5.2 0.7 copy-done.4
  5.8 81.6 %lamb.1 = (f32[64,128]{1,0:T(8,128)S(1)}, f32[64,128]{1,0:T(8,128)S(1)}, f32[64,128]{1,0:T(8,128)S(1)}, bf16[4096,128]{1,0:T(8,128)(2,1)S(1)}) custom-call(s32[40]{0:T(128)S(1)} %copy-done.4, s32[1,128]{1,0:T(1,128)S(1)} %pad_bitcast_fusion.flags, f32[4096,128]{1,0:T(8,128)S(1)} %bitcast.14, f32[64,128]{1,0:T(8,128)S(1)} %bitcast.16, ...), custom_call_target="tpu_custom_call" | custom-call | tf_op jit(solution)/shard_map/lamb/pallas_call | solution.py:362
  87.4 17.0 %copy.12 = bf16[1,1,4096,128]{3,1,2,0:T(2,128)(2,1)} copy(bf16[1,1,4096,128]{3,2,1,0:T(8,128)(2,1)S(1)} %bitcast.15) | data formatting | bytes 2097152
  104.4 0.6 copy.16
  105.0 0.6 copy.17
  105.6 0.6 copy.18
Async XLA Ops:
  1.3 1.6 %copy-start = (f32[1,1,524288]{2,1,0:T(1,128)S(1)}, f32[1,1,524288]{2,1,0:T(1,128)}, u32[]{:S(2)}) copy-start(f32[1,1,524288]{2,1,0:T(1,128)} %param.6) | copy-start | bytes 6291460
  2.9 0.8 copy-start.1
  3.6 0.8 copy-start.2
  4.4 0.8 copy-start.3
  5.2 0.7 copy-start.4

commit v2 on v1

--- a/solution.py
+++ b/solution.py
@@ -6,7 +6,7 @@
 from jax.sharding import PartitionSpec as P
 
 MESH = pl.DeviceIdType.MESH
-NZ, NX, NT = 16, 4, 8
+NZ, NX, NY, NT = 16, 4, 4, 8
 GROUP = 4
 ROWS = 64
 WORDS = 32
@@ -29,6 +29,10 @@
     low = ((words << 16) >> 16).astype(jnp.float32) * step
     return high, low
 
+
+LONG = (8, 4, 12)
+SHORT = (2, 1, 15)
+ARRIVALS = (1, 15, 2, 4, 12, 5, 11, 3, 13, 6, 14, 8, 7, 9, 10)
 
 UNIT_X = float(2**26)
 UNIT_Z = float(2**24)
@@ -47,10 +51,10 @@
 
 
 def kernel(
-    lengths, flags, grads, master, avg, avg_sq,
-    out_master, out_avg, out_avg_sq, out_model,
-    held, coded, x_in, z_out, z_in, total, state, stat_z, stat_p, weights,
-    load_sem, state_sem, xs_sem, xr_sem, zs_sem, zr_sem, ns_sem, nr_sem, ps_sem, pr_sem,
+    lengths_in, flags_in, grads, master, avg, avg_sq,
+    out_master, out_avg, out_avg_sq, weights,
+    held, coded, x_in, z_out, z_in, total, state, made, stat_z, stat_p, lengths, flags,
+    word_sem, load_sem, state_sem, out_sem, xs_sem, xr_sem, zs_sem, zr_sem, ns_sem, nr_sem, ps_sem, pr_sem,
     gs_sem, gr_sem, fs_sem, fr_sem,
 ):
     dp = lax.axis_index("dp")
@@ -74,28 +78,38 @@
         pltpu.make_async_copy(ref, state.at[i], state_sem.at[i])
         for i, ref in enumerate((master, avg, avg_sq))
     ]
+    state_copies += [
+        pltpu.make_async_copy(lengths_in, lengths, state_sem.at[3]),
+        pltpu.make_async_copy(flags_in, flags, state_sem.at[4]),
+    ]
     for copy in state_copies:
         copy.start()
+    out_copies = [
+        pltpu.make_async_copy(made.at[i], ref, out_sem.at[i])
+        for i, ref in enumerate((out_master, out_avg, out_avg_sq))
+    ]
 
     barrier = pltpu.get_barrier_semaphore()
 
-    def hail_z(o, c):
-        pl.semaphore_signal(barrier, 1, device_id=at((z + o) % NZ, x, t), device_id_type=MESH)
-        return c
-
-    lax.fori_loop(1, NZ, hail_z, 0)
-
-    def plane(o):
-        me = x * NT + t
-        other = (me + o) % (NX * NT)
-        return other // NT, other % NT
-
-    def hail_p(o, c):
-        xx, tt = plane(o)
-        pl.semaphore_signal(barrier, 1, device_id=at(z, xx, tt), device_id_type=MESH)
-        return c
-
-    lax.fori_loop(1, NX * NT, hail_p, 0)
+    y, core = t // 2, t % 2
+
+    def near(dx, dy, dc):
+        return at(z, (x + dx) % NX, ((y + dy) % NY) * 2 + (core + dc) % 2)
+
+    greeted = [near(dx, 0, 0) for dx in range(1, NX)]
+    greeted += [near(0, dy, dc) for dy in range(NY) for dc in range(2) if dy or dc]
+    greeted += [at((z + o) % NZ, x, t) for o in (1, NZ - 1)]
+    for device in greeted:
+        pl.semaphore_signal(barrier, 1, device_id=device, device_id_type=MESH)
+
+    def pass_on(step):
+        for o in (2**step, NZ - 2**step):
+            pl.semaphore_signal(
+                word_sem.at[step], 1, device_id=at((z + o) % NZ, x, t), device_id_type=MESH
+            )
+
+    def hear(step):
+        pl.semaphore_wait(word_sem.at[step], 2)
 
     def x_copy(k, o):
         a = group_of(k)
@@ -130,20 +144,26 @@
 
         lax.fori_loop(1, NX, code, 0)
         if n == 0:
-            pl.semaphore_wait(barrier, NZ - 1 + NX * NT - 1)
+            pl.semaphore_wait(barrier, len(greeted))
         for o in (2, 1, 3):
             x_copy(k, o).start()
-
+        if n > 0:
+            hear(n - 1)
+        if n < 3:
+            pass_on(n)
+
+    for copy in state_copies:
+        copy.wait()
     starts = [jnp.int32(0)]
+    split = jnp.zeros((1, 128), jnp.int32)
     for k in range(NP):
         starts.append(starts[-1] + lengths[k])
+        split = jnp.where(lax.broadcasted_iota(jnp.int32, (1, 128), 1) == k, flags[k], split)
     position = (
         dp * (ROWS * 128)
         + lax.broadcasted_iota(jnp.int32, (ROWS, 128), 0) * 128
         + lax.broadcasted_iota(jnp.int32, (ROWS, 128), 1)
     )
-    for copy in state_copies:
-        copy.wait()
     w = state[0]
     w_sums = piece_sums(w * w, position, starts)
 
@@ -208,8 +228,10 @@
     grad = total[...] * (1.0 / (NZ * NX))
     new_avg = 0.9 * state[1] + 0.1 * grad
     new_avg_sq = 0.95 * state[2] + 0.05 * grad * grad
-    out_avg[...] = new_avg
-    out_avg_sq[...] = new_avg_sq
+    made[1] = new_avg
+    made[2] = new_avg_sq
+    out_copies[1].start()
+    out_copies[2].start()
     update = new_avg / (jnp.sqrt(new_avg_sq) + 1e-08) + 0.1 * state[0]
     total[...] = update
     u_sums = piece_sums(update * update, position, starts)
@@ -243,114 +265,112 @@
     me = x * NT + t
     stat_p[me, 0:2, :] = sums
 
-    def p_copy(o):
-        xx, tt = plane(o)
+    plane = [
+        (dx, dy, dc) for dx in (2, 1, 3, 0) for dy in (2, 1, 3, 0) for dc in (1, 0) if dx or dy or dc
+    ]
+
+    def p_copy(n):
         return pltpu.make_async_remote_copy(
             src_ref=stat_p.at[me, pl.ds(0, 2)], dst_ref=stat_p.at[me, pl.ds(0, 2)],
-            send_sem=ps_sem.at[o], recv_sem=pr_sem.at[me],
-            device_id=at(z, xx, tt), device_id_type=MESH,
-        )
-
-    def p_arrival(o):
-        xx, tt = plane(o)
-        return pltpu.make_async_remote_copy(
-            src_ref=stat_p.at[me, pl.ds(0, 2)], dst_ref=stat_p.at[xx * NT + tt, pl.ds(0, 2)],
-            send_sem=ps_sem.at[o], recv_sem=pr_sem.at[xx * NT + tt],
-            device_id=at(z, xx, tt), device_id_type=MESH,
-        )
-
-    def start_p(o, c):
-        p_copy(o).start()
-        return c
-
-    def wait_p(o, c):
-        p_arrival(o).wait_recv()
-        return c
-
-    lax.fori_loop(1, NX * NT, start_p, 0)
-    lax.fori_loop(1, NX * NT, wait_p, 0)
+            send_sem=ps_sem.at[n], recv_sem=pr_sem.at[me],
+            device_id=near(*plane[n]), device_id_type=MESH,
+        )
+
+    def p_arrival(n):
+        dp_there, t_there = near(*plane[n])
+        slot = (dp_there - z * NX) * NT + t_there
+        return pltpu.make_async_remote_copy(
+            src_ref=stat_p.at[me, pl.ds(0, 2)], dst_ref=stat_p.at[slot, pl.ds(0, 2)],
+            send_sem=ps_sem.at[n], recv_sem=pr_sem.at[slot],
+            device_id=near(*plane[n]), device_id_type=MESH,
+        )
+
+    for n in range(NX * NT - 1):
+        p_copy(n).start()
+    for n in range(NX * NT - 1):
+        p_arrival(n).wait_recv()
     data_sum = stat_p[t, 0:2, :]
     for xx in range(1, NX):
         data_sum = data_sum + stat_p[xx * NT + t, 0:2, :]
     tensor_sum = stat_p[0, 0:2, :]
     for i in range(1, NX * NT):
         tensor_sum = tensor_sum + stat_p[i, 0:2, :]
-    effective = jnp.where(flags[0:1, :] == 1, tensor_sum, data_sum)
+    effective = jnp.where(split == 1, tensor_sum, data_sum)
     trust = jnp.sqrt(effective[0:1]) / jnp.maximum(jnp.sqrt(effective[1:2]), 1.0)
     trust_at = jnp.broadcast_to(trust[:, 0:1], (ROWS, 128))
     for k in range(1, NP):
         trust_at = jnp.where(position >= starts[k], trust[:, k : k + 1], trust_at)
     new_weights = state[0] - 0.05 * trust_at * total[...]
-    out_master[...] = new_weights
 
     weights[z, x] = new_weights.astype(jnp.bfloat16)
 
-    def g_copy(o):
-        zz = (z + o) % NZ
-        return pltpu.make_async_remote_copy(
-            src_ref=weights.at[z, x], dst_ref=weights.at[z, x],
-            send_sem=gs_sem.at[o], recv_sem=gr_sem.at[z],
-            device_id=at(zz, x, t), device_id_type=MESH,
-        )
-
-    def g_arrival(zz):
-        return pltpu.make_async_remote_copy(
-            src_ref=weights.at[z, x], dst_ref=weights.at[zz, x],
-            send_sem=gs_sem.at[1], recv_sem=gr_sem.at[zz],
-            device_id=at(zz, x, t), device_id_type=MESH,
-        )
-
-    for o in (8, 7, 9, 6, 10, 5, 11, 4, 12, 3, 13, 2, 14, 1, 15):
-        g_copy(o).start()
-
-    def f_copy(k, o):
-        a = group_of(k)
-        xx = (x + o) % NX
-        blocks = weights.at[pl.ds(a * GROUP, GROUP), x]
-        return pltpu.make_async_remote_copy(
-            src_ref=blocks, dst_ref=blocks,
-            send_sem=fs_sem.at[o, k], recv_sem=fr_sem.at[x, a],
+    def g_copy(back, o):
+        block = weights.at[(z - back) % NZ, x]
+        return pltpu.make_async_remote_copy(
+            src_ref=block, dst_ref=block,
+            send_sem=gs_sem.at[back, o], recv_sem=gr_sem.at[(z - back) % NZ],
+            device_id=at((z + o) % NZ, x, t), device_id_type=MESH,
+        )
+
+    def f_copy(back, dx):
+        block = weights.at[(z - back) % NZ, x]
+        return pltpu.make_async_remote_copy(
+            src_ref=block, dst_ref=block,
+            send_sem=fs_sem.at[back, dx], recv_sem=fr_sem.at[x, (z - back) % NZ],
+            device_id=at(z, (x + dx) % NX, t), device_id_type=MESH,
+        )
+
+    def f_arrival(back, dx):
+        xx = (x + dx) % NX
+        block = weights.at[(z - back) % NZ, xx]
+        return pltpu.make_async_remote_copy(
+            src_ref=block, dst_ref=block,
+            send_sem=fs_sem.at[back, dx], recv_sem=fr_sem.at[xx, (z - back) % NZ],
             device_id=at(z, xx, t), device_id_type=MESH,
         )
 
-    def f_arrival(k, o):
-        a = group_of(k)
-        xx = (x + o) % NX
-        blocks = weights.at[pl.ds(a * GROUP, GROUP), xx]
-        return pltpu.make_async_remote_copy(
-            src_ref=blocks, dst_ref=blocks,
-            send_sem=fs_sem.at[o, k], recv_sem=fr_sem.at[xx, a],
-            device_id=at(z, xx, t), device_id_type=MESH,
-        )
-
-    for k in (0, 1, 3, 2):
-        for i in range(1 if k == 0 else 0, GROUP):
-            g_arrival(group_of(k) * GROUP + (z + i) % GROUP).wait_recv()
-        for o in (2, 1, 3):
-            f_copy(k, o).start()
-    for k in (0, 1, 3, 2):
-        for o in (1, 3, 2):
-            f_arrival(k, o).wait_recv()
-        a = group_of(k)
-        for j in range(GROUP):
-            for xx in range(NX):
-                start = pl.multiple_of(((a * GROUP + j) * NX + xx) * ROWS, ROWS)
-                out_model[pl.ds(start, ROWS), :] = weights[a * GROUP + j, xx]
-
+    def relay(back):
+        for o in SHORT:
+            g_copy(back, o).start()
+
+    def spread(back):
+        for dx in (2, 1, 3):
+            f_copy(back, dx).start()
+
+    for o in LONG:
+        g_copy(0, o).start()
+    relay(0)
+    spread(0)
+    made[0] = new_weights
+    out_copies[0].start()
+
+    for back in ARRIVALS:
+        g_copy(back, 1).wait_recv()
+        if back in LONG:
+            relay(back)
+        spread(back)
+    for back in (0, *ARRIVALS):
+        for dx in (1, 3, 2):
+            f_arrival(back, dx).wait_recv()
+
+    for copy in out_copies:
+        copy.wait()
     for k in ORDER:
         for o in range(1, NX):
             x_copy(k, o).wait_send()
-            f_copy(k, o).wait_send()
     for o in range(1, NZ):
         z_copy((z + o) % NZ).wait_send()
         n_copy(o).wait_send()
-        g_copy(o).wait_send()
-
-    def end_p(o, c):
-        p_copy(o).wait_send()
-        return c
-
-    lax.fori_loop(1, NX * NT, end_p, 0)
+    for n in range(NX * NT - 1):
+        p_copy(n).wait_send()
+    for o in LONG:
+        g_copy(0, o).wait_send()
+    for back in (0, *LONG):
+        for o in SHORT:
+            g_copy(back, o).wait_send()
+    for back in range(NZ):
+        for dx in range(1, NX):
+            f_copy(back, dx).wait_send()
 
 
 def local(grads, piece_lengths, split_flags, master_params, exp_avg, exp_avg_sq):
@@ -358,13 +378,13 @@
     anywhere = pl.BlockSpec(memory_space=pltpu.HBM)
     shard = jax.ShapeDtypeStruct((ROWS, 128), jnp.float32)
     dma = pltpu.SemaphoreType.DMA
-    flags = jnp.pad(split_flags, (0, 128 - NP)).reshape(1, 128)
+    hbm = lambda array: pltpu.with_memory_space_constraint(array, pltpu.HBM)
     new_master, new_avg, new_avg_sq, model = pl.pallas_call(
         kernel,
         name="lamb",
-        out_shape=(shard, shard, shard, jax.ShapeDtypeStruct((NZ * NX * ROWS, 128), jnp.bfloat16)),
-        in_specs=[pl.BlockSpec(memory_space=pltpu.SMEM), vmem, anywhere, anywhere, anywhere, anywhere],
-        out_specs=(vmem, vmem, vmem, vmem),
+        out_shape=(shard, shard, shard, jax.ShapeDtypeStruct((NZ, NX, ROWS, 128), jnp.bfloat16)),
+        in_specs=[anywhere] * 6,
+        out_specs=(anywhere, anywhere, anywhere, vmem),
         scratch_shapes=[
             pltpu.VMEM((NZ * NX * ROWS, 128), jnp.float32),
             pltpu.VMEM((NX, GROUP, XROWS, 128), jnp.int32),
@@ -373,24 +393,27 @@
             pltpu.VMEM((NZ, WORDS + 8, 128), jnp.int32),
             pltpu.VMEM((ROWS, 128), jnp.float32),
             pltpu.VMEM((3, ROWS, 128), jnp.float32),
+            pltpu.VMEM((3, ROWS, 128), jnp.float32),
             pltpu.VMEM((NZ, 8, 128), jnp.float32),
             pltpu.VMEM((NX * NT, 8, 128), jnp.float32),
-            pltpu.VMEM((NZ, NX, ROWS, 128), jnp.bfloat16),
-            dma((4,)), dma((3,)),
+            pltpu.SMEM((NP,), jnp.int32),
+            pltpu.SMEM((NP,), jnp.int32),
+            pltpu.SemaphoreType.REGULAR((3,)), dma((4,)), dma((5,)), dma((3,)),
             dma((NX, 4)), dma((NX, 4)),
             dma((NZ,)), dma((NZ,)),
             dma((NZ,)), dma((NZ,)),
             dma((NX * NT,)), dma((NX * NT,)),
-            dma((NZ,)), dma((NZ,)),
-            dma((NX, 4)), dma((NX, 4)),
+            dma((NZ, NZ)), dma((NZ,)),
+            dma((NZ, NX)), dma((NX, NZ)),
         ],
         compiler_params=pltpu.CompilerParams(
             collective_id=0, has_side_effects=True, vmem_limit_bytes=24 * 2**20
         ),
     )(
-        piece_lengths, flags, grads.reshape(NZ * NX * ROWS, 128), master_params.reshape(ROWS, 128),
-        exp_avg.reshape(ROWS, 128), exp_avg_sq.reshape(ROWS, 128),
+        hbm(piece_lengths), hbm(split_flags), hbm(grads.reshape(NZ * NX * ROWS, 128)),
+        hbm(master_params.reshape(ROWS, 128)), hbm(exp_avg.reshape(ROWS, 128)), hbm(exp_avg_sq.reshape(ROWS, 128)),
     )
+    model = lax.optimization_barrier(model.reshape(-1))
     return (
         new_master.reshape(1, -1), new_avg.reshape(1, -1), new_avg_sq.reshape(1, -1), model.reshape(1, -1)
     )

time: 107 us -> 76.6 us (0.72)
  the two profiles are of different devices: /device:TPU:1 before, /device:TPU:6 now
where the time goes in v2:
time: 76.6 us; the launch traced here: 75.3 us
  Pallas kernels  70.4 us (92%)
  local copies, waits for them, and re-layouts  4.28 us (6%)
    pallas_call x1, Pallas kernels, local(): pl.pallas_call(kernel, name='lamb', out_shape=(shard, shard, shard, jax.S...  70.4 us
    reshape x1, local copies, waits for them, and re-layouts, local(): model.reshape(1, -1)  2.43 us
    unnamed x3, local copies, waits for them, and re-layouts  1.84 us

profile of v2, /device:TPU:6, one launch (start us, length us, event | category | flops | bytes accessed | tf_op | source)
XLA Modules:
  0.0 75.3 jit_solution(14138810372121079176)
XLA Ops:
  0.6 70.4 %lamb.1 = (f32[64,128]{1,0:T(8,128)S(1)}, f32[64,128]{1,0:T(8,128)S(1)}, f32[64,128]{1,0:T(8,128)S(1)}, bf16[16,4,64,128]{3,2,1,0:T(8,128)(2,1)S(1)}) custom-call(s32[40]{0:T(128)} %lengths_in.1, s32[40]{0:T(128)} %flags_in.1, f32[4096,128]{1,0:T(8,128)} %bitcast.12, f32[64,128]{1,0:T(8,128)} %bitcast.13, f32[64,128]{1,0:T(8,128)} %bitcast.14, ...), custom_call_target="tpu_custom_call" | custom-call | tf_op jit(solution)/shard_map/lamb/pallas_call | solution.py:382
  71.0 2.4 %reshape.43 = bf16[1,524288]{1,0:T(2,128)(2,1)} reshape(bf16[524288]{0:T(1024)(128)(2,1)S(1)} %bitcast.8) | data formatting | bytes 2097152 | tf_op jit(solution)/shard_map/reshape | solution.py:418
  73.4 0.6 copy.13
  74.1 0.6 copy.14
  74.7 0.6 copy.15

commit v3 on v2

v3 whole, which is shorter than its diff:
```python
import jax
import jax.numpy as jnp
from jax import lax
from jax.experimental import pallas as pl
from jax.experimental.pallas import tpu as pltpu
from jax.sharding import PartitionSpec as P

MESH = pl.DeviceIdType.MESH
NZ, NX, NY, NT = 16, 4, 4, 8
ROWS = 64
WORDS = 32
NP = 40
CODED = WORDS + 1


def encode(block, unit):
    top = jnp.max(jnp.abs(block), axis=0, keepdims=True)
    scale = (top * unit).astype(jnp.int32) + 1
    inverse = (32767.0 * unit) / scale.astype(jnp.float32)
    codes = jnp.round(block * inverse).astype(jnp.int32)
    return (codes[:WORDS] << 16) + codes[WORDS:], scale


def decode(words, scale, unit):
    step = scale.astype(jnp.float32) * (1.0 / (32767.0 * unit))
    high = ((words + 32768) >> 16).astype(jnp.float32) * step
    low = ((words << 16) >> 16).astype(jnp.float32) * step
    return high, low


NEAR = (2, 14, 1, 15)
LONG = (8, 5, 11, 3, 13)
RELAYS = {3: (1,), 13: (15,), 5: (2, 1), 11: (14, 15), 8: ()}
ARRIVALS = (3, 13, 5, 11, 4, 12, 8, 6, 10, 7, 9)
FAR_FIRST = (8, 7, 9, 6, 10, 5, 11, 4, 12, 3, 13, 2, 14, 1, 15)

UNIT_X = float(2**26)
UNIT_Z = float(2**24)


def piece_sums(values, position, starts):
    rows = []
    for k in range(NP):
        inside = (position >= starts[k]) & (position < starts[k + 1])
        rows.append(jnp.sum(jnp.where(inside, values, 0.0), axis=0, keepdims=True))
    table = jnp.concatenate(rows, axis=0)
    totals = jnp.sum(table, axis=1, keepdims=True)
    piece = lax.broadcasted_iota(jnp.int32, (NP, 128), 0)
    lane = lax.broadcasted_iota(jnp.int32, (NP, 128), 1)
    return jnp.sum(jnp.where(piece == lane, totals, 0.0), axis=0, keepdims=True)


def kernel(
    lengths_in, flags_in, grads, master, avg, avg_sq,
    made, weights,
    held, coded, x_in, z_out, z_in, total, state, stat_z, stat_p, lengths, flags,
    word_sem, load_sem, state_sem, xs_sem, xr_sem, zs_sem, zr_sem, ns_sem, nr_sem, ps_sem, pr_sem,
    gs_sem, gr_sem, rs_sem, rr_sem, fs_sem, fr_sem,
):
    dp = lax.axis_index("dp")
    t = lax.axis_index("tensor")
    z, x = dp // NX, dp % NX

    def at(zz, xx, tt):
        return (zz * NX + xx, tt)

    def load(zz):
        rows = pl.ds(pl.multiple_of(zz * (NX * ROWS), NX * ROWS), NX * ROWS)
        return pltpu.make_async_copy(grads.at[rows], held.at[rows], load_sem.at[zz])

    for o in (*FAR_FIRST, 0):
        load((z + o) % NZ).start()
    state_copies = [
        pltpu.make_async_copy(ref, state.at[i], state_sem.at[i])
        for i, ref in enumerate((master, avg, avg_sq))
    ]
    state_copies += [
        pltpu.make_async_copy(lengths_in, lengths, state_sem.at[3]),
        pltpu.make_async_copy(flags_in, flags, state_sem.at[4]),
    ]
    for copy in state_copies:
        copy.start()

    barrier = pltpu.get_barrier_semaphore()

    y, core = t // 2, t % 2

    def near(dx, dy, dc):
        return at(z, (x + dx) % NX, ((y + dy) % NY) * 2 + (core + dc) % 2)

    greeted = [near(dx, 0, 0) for dx in range(1, NX)]
    greeted += [near(0, dy, dc) for dy in range(NY) for dc in range(2) if dy or dc]
    greeted += [at((z + o) % NZ, x, t) for o in (1, 15, 2, 14, 3, 13, 4, 12)]
    for device in greeted:
        pl.semaphore_signal(barrier, 1, device_id=device, device_id_type=MESH)

    def far(i):
        return jnp.where(i % 2 == 0, NZ // 2 + i // 2, NZ // 2 - (i + 1) // 2)

    def x_copy(zz, dx):
        xx = (x + dx) % NX
        return pltpu.make_async_remote_copy(
            src_ref=coded.at[xx, zz, pl.ds(0, CODED)], dst_ref=x_in.at[x, zz, pl.ds(0, CODED)],
            send_sem=xs_sem.at[dx, zz], recv_sem=xr_sem.at[x, zz],
            device_id=at(z, xx, t), device_id_type=MESH,
        )

    def x_arrival(zz, dx):
        xx = (x + dx) % NX
        return pltpu.make_async_remote_copy(
            src_ref=coded.at[xx, zz, pl.ds(0, CODED)], dst_ref=x_in.at[xx, zz, pl.ds(0, CODED)],
            send_sem=xs_sem.at[dx, zz], recv_sem=xr_sem.at[xx, zz],
            device_id=at(z, xx, t), device_id_type=MESH,
        )

    pl.semaphore_wait(barrier, len(greeted))
    for o in (4, 12):
        pl.semaphore_signal(word_sem, 1, device_id=at((z + o) % NZ, x, t), device_id_type=MESH)

    def scatter(i, c):
        zz = (z + far(i)) % NZ
        load(zz).wait()
        for dx in (2, 1, 3):
            xx = (x + dx) % NX
            start = pl.multiple_of((zz * NX + xx) * ROWS, ROWS)
            words, scale = encode(held[pl.ds(start, ROWS), :], UNIT_X)
            coded[xx, zz, :WORDS, :] = words
            coded[xx, zz, WORDS:CODED, :] = scale
            x_copy(zz, dx).start()
        return c

    lax.fori_loop(0, NZ, scatter, 0)

    for copy in state_copies:
        copy.wait()
    starts = [jnp.int32(0)]
    split = jnp.zeros((1, 128), jnp.int32)
    for k in range(NP):
        starts.append(starts[-1] + lengths[k])
        split = jnp.where(lax.broadcasted_iota(jnp.int32, (1, 128), 1) == k, flags[k], split)
    position = (
        dp * (ROWS * 128)
        + lax.broadcasted_iota(jnp.int32, (ROWS, 128), 0) * 128
        + lax.broadcasted_iota(jnp.int32, (ROWS, 128), 1)
    )
    w = state[0]
    w_sums = piece_sums(w * w, position, starts)

    def z_copy(zz):
        return pltpu.make_async_remote_copy(
            src_ref=z_out.at[zz, pl.ds(0, CODED)], dst_ref=z_in.at[z, pl.ds(0, CODED)],
            send_sem=zs_sem.at[zz], recv_sem=zr_sem.at[z],
            device_id=at(zz, x, t), device_id_type=MESH,
        )

    def z_arrival(zz):
        return pltpu.make_async_remote_copy(
            src_ref=z_out.at[zz, pl.ds(0, CODED)], dst_ref=z_in.at[zz, pl.ds(0, CODED)],
            send_sem=zs_sem.at[zz], recv_sem=zr_sem.at[zz],
            device_id=at(zz, x, t), device_id_type=MESH,
        )

    def sum_over_x(zz):
        start = pl.multiple_of((zz * NX + x) * ROWS, ROWS)
        high = held[pl.ds(start, WORDS), :]
        low = held[pl.ds(pl.multiple_of(start + WORDS, WORDS), WORDS), :]
        for dx in (1, 3, 2):
            xx = (x + dx) % NX
            x_arrival(zz, dx).wait_recv()
            h, l = decode(x_in[xx, zz, :WORDS, :], x_in[xx, zz, WORDS:CODED, :], UNIT_X)
            high, low = high + h, low + l
        return high, low

    def forward(i, c):
        zz = (z + far(i)) % NZ
        high, low = sum_over_x(zz)
        words, scale = encode(jnp.concatenate([high, low], axis=0), UNIT_Z)
        z_out[zz, :WORDS, :] = words
        z_out[zz, WORDS:CODED, :] = scale
        z_copy(zz).start()
        return c

    pl.semaphore_wait(word_sem, 2)
    lax.fori_loop(0, NZ - 1, forward, 0)
    high, low = sum_over_x(z)
    total[:WORDS, :] = high
    total[WORDS:, :] = low

    def collect(o, c):
        zz = (z + o) % NZ
        z_arrival(zz).wait_recv()
        h, l = decode(z_in[zz, :WORDS, :], z_in[zz, WORDS:CODED, :], UNIT_Z)
        total[:WORDS, :] += h
        total[WORDS:, :] += l
        return c

    lax.fori_loop(1, NZ, collect, 0)

    grad = total[...] * (1.0 / (NZ * NX))
    new_avg = 0.9 * state[1] + 0.1 * grad
    new_avg_sq = 0.95 * state[2] + 0.05 * grad * grad
    made[1] = new_avg
    made[2] = new_avg_sq
    update = new_avg / (jnp.sqrt(new_avg_sq) + 1e-08) + 0.1 * state[0]
    total[...] = update
    u_sums = piece_sums(update * update, position, starts)

    mine = z * 2 + core
    stat_z[mine, 0:1, :] = w_sums
    stat_z[mine, 1:2, :] = u_sums
    line = [(o, dc) for o in FAR_FIRST for dc in (1, 0)] + [(0, 1)]

    def n_copy(n, slot=mine):
        o, dc = line[n]
        return pltpu.make_async_remote_copy(
            src_ref=stat_z.at[mine, pl.ds(0, 2)], dst_ref=stat_z.at[slot, pl.ds(0, 2)],
            send_sem=ns_sem.at[n], recv_sem=nr_sem.at[slot],
            device_id=at((z + o) % NZ, x, y * 2 + (core + dc) % 2), device_id_type=MESH,
        )

    def n_arrival(n):
        o, dc = line[n]
        return n_copy(n, ((z + o) % NZ) * 2 + (core + dc) % 2)

    for n in range(len(line)):
        n_copy(n).start()
    for n in reversed(range(len(line))):
        n_arrival(n).wait_recv()
    own = stat_z[core, 0:2, :]
    other = stat_z[1 - core, 0:2, :]
    for zz in range(1, NZ):
        own = own + stat_z[zz * 2 + core, 0:2, :]
        other = other + stat_z[zz * 2 + 1 - core, 0:2, :]
    me = x * NY + y
    stat_p[me, 0:2, :] = own
    stat_p[me, 2:4, :] = own + other
    plane = [(dx, dy) for dx in (2, 1, 3, 0) for dy in (2, 1, 3, 0) if dx or dy]

    def p_copy(n, slot=me):
        dx, dy = plane[n]
        return pltpu.make_async_remote_copy(
            src_ref=stat_p.at[me, pl.ds(0, 4)], dst_ref=stat_p.at[slot, pl.ds(0, 4)],
            send_sem=ps_sem.at[n], recv_sem=pr_sem.at[slot],
            device_id=near(dx, dy, 0), device_id_type=MESH,
        )

    def p_arrival(n):
        dx, dy = plane[n]
        return p_copy(n, ((x + dx) % NX) * NY + (y + dy) % NY)

    for n in range(len(plane)):
        p_copy(n).start()
    for n in reversed(range(len(plane))):
        p_arrival(n).wait_recv()
    data_sum = stat_p[y, 0:2, :]
    for xx in range(1, NX):
        data_sum = data_sum + stat_p[xx * NY + y, 0:2, :]
    tensor_sum = stat_p[0, 2:4, :]
    for i in range(1, NX * NY):
        tensor_sum = tensor_sum + stat_p[i, 2:4, :]
    effective = jnp.where(split == 1, tensor_sum, data_sum)
    trust = jnp.sqrt(effective[0:1]) / jnp.maximum(jnp.sqrt(effective[1:2]), 1.0)
    trust_at = jnp.broadcast_to(trust[:, 0:1], (ROWS, 128))
    for k in range(1, NP):
        trust_at = jnp.where(position >= starts[k], trust[:, k : k + 1], trust_at)
    new_weights = state[0] - 0.05 * trust_at * total[...]

    weights[z, x] = new_weights.astype(jnp.bfloat16)

    def g_copy(back, o):
        block = weights.at[(z - back) % NZ, x]
        return pltpu.make_async_remote_copy(
            src_ref=block, dst_ref=block,
            send_sem=gs_sem.at[back, o], recv_sem=gr_sem.at[(z - back) % NZ],
            device_id=at((z + o) % NZ, x, t), device_id_type=MESH,
        )

    def f_copy(back, dx):
        block = weights.at[(z - back) % NZ, x]
        return pltpu.make_async_remote_copy(
            src_ref=block, dst_ref=block,
            send_sem=fs_sem.at[back, dx], recv_sem=fr_sem.at[x, (z - back) % NZ],
            device_id=at(z, (x + dx) % NX, t), device_id_type=MESH,
        )

    def f_arrival(back, dx):
        xx = (x + dx) % NX
        block = weights.at[(z - back) % NZ, xx]
        return pltpu.make_async_remote_copy(
            src_ref=block, dst_ref=block,
            send_sem=fs_sem.at[back, dx], recv_sem=fr_sem.at[xx, (z - back) % NZ],
            device_id=at(z, xx, t), device_id_type=MESH,
        )

    def r_copy(o, row=z):
        return pltpu.make_async_remote_copy(
            src_ref=weights.at[row], dst_ref=weights.at[row],
            send_sem=rs_sem.at[o], recv_sem=rr_sem.at[row],
            device_id=at((z + o) % NZ, x, t), device_id_type=MESH,
        )

    def spread(back):
        for dx in (2, 1, 3):
            f_copy(back, dx).start()

    for o in LONG:
        g_copy(0, o).start()
    spread(0)
    made[0] = new_weights

    for o in range(1, NZ):
        for dx in range(1, NX):
            x_copy((z + o) % NZ, dx).wait_send()
        z_copy((z + o) % NZ).wait_send()
    for dx in range(1, NX):
        x_copy(z, dx).wait_send()
    for n in range(len(line)):
        n_copy(n).wait_send()
    for n in range(len(plane)):
        p_copy(n).wait_send()

    for back in ARRIVALS:
        g_copy(back, 1).wait_recv()
        for o in RELAYS.get(back, ()):
            g_copy(back, o).start()
        spread(back)
        if back == 11:
            for dx in (1, 3, 2):
                f_arrival(0, dx).wait_recv()
            for o in NEAR:
                r_copy(o).start()
    for o in NEAR:
        r_copy(o, (z + o) % NZ).wait_recv()
    for back in ARRIVALS:
        for dx in (1, 3, 2):
            f_arrival(back, dx).wait_recv()

    for o in NEAR:
        r_copy(o).wait_send()
    for o in LONG:
        g_copy(0, o).wait_send()
        for far_o in RELAYS[o]:
            g_copy(o, far_o).wait_send()
    for back in (0, *ARRIVALS):
        for dx in range(1, NX):
            f_copy(back, dx).wait_send()


def local(grads, piece_lengths, split_flags, master_params, exp_avg, exp_avg_sq):
    vmem = pl.BlockSpec(memory_space=pltpu.VMEM)
    anywhere = pl.BlockSpec(memory_space=pltpu.HBM)
    dma = pltpu.SemaphoreType.DMA
    hbm = lambda array: pltpu.with_memory_space_constraint(array, pltpu.HBM)
    made, model = pl.pallas_call(
        kernel,
        name="lamb",
        out_shape=(jax.ShapeDtypeStruct((3, ROWS, 128), jnp.float32), jax.ShapeDtypeStruct((NZ, NX, ROWS, 128), jnp.bfloat16)),
        in_specs=[anywhere] * 6,
        out_specs=(vmem, vmem),
        scratch_shapes=[
            pltpu.VMEM((NZ * NX * ROWS, 128), jnp.float32),
            pltpu.VMEM((NX, NZ, WORDS + 8, 128), jnp.int32),
            pltpu.VMEM((NX, NZ, WORDS + 8, 128), jnp.int32),
            pltpu.VMEM((NZ, WORDS + 8, 128), jnp.int32),
            pltpu.VMEM((NZ, WORDS + 8, 128), jnp.int32),
            pltpu.VMEM((ROWS, 128), jnp.float32),
            pltpu.VMEM((3, ROWS, 128), jnp.float32),
            pltpu.VMEM((NZ * 2, 8, 128), jnp.float32),
            pltpu.VMEM((NX * NY, 8, 128), jnp.float32),
            pltpu.SMEM((NP,), jnp.int32),
            pltpu.SMEM((NP,), jnp.int32),
            pltpu.SemaphoreType.REGULAR, dma((NZ,)), dma((5,)),
            dma((NX, NZ)), dma((NX, NZ)),
            dma((NZ,)), dma((NZ,)),
            dma((NZ * 2,)), dma((NZ * 2,)),
            dma((NX * NY,)), dma((NX * NY,)),
            dma((NZ, NZ)), dma((NZ,)),
            dma((NZ,)), dma((NZ,)),
            dma((NZ, NX)), dma((NX, NZ)),
        ],
        compiler_params=pltpu.CompilerParams(
            collective_id=0, has_side_effects=True, vmem_limit_bytes=24 * 2**20
        ),
    )(
        hbm(piece_lengths), hbm(split_flags), hbm(grads.reshape(NZ * NX * ROWS, 128)),
        hbm(master_params.reshape(ROWS, 128)), hbm(exp_avg.reshape(ROWS, 128)), hbm(exp_avg_sq.reshape(ROWS, 128)),
    )
    model = lax.optimization_barrier(model.reshape(-1))
    return (
        made[0].reshape(1, -1), made[1].reshape(1, -1), made[2].reshape(1, -1), model.reshape(1, -1)
    )


def solution(mesh):
    return jax.shard_map(
        local,
        mesh=mesh,
        in_specs=(
            P("dp", "tensor", None),
            P(),
            P(),
            P("tensor", "dp"),
            P("tensor", "dp"),
            P("tensor", "dp"),
        ),
        out_specs=(P("tensor", "dp"), P("tensor", "dp"), P("tensor", "dp"), P("tensor", None)),
        check_vma=False,
    )
```

time: 76.6 us -> 69.6 us (0.909); the launches traced: 75.3 us -> 69.1 us
  Pallas kernels: 70.4 us -> 65.4 us
  local copies, waits for them, and re-layouts: 4.28 us -> 3.05 us
    pallas_call x1, Pallas kernels: 70.4 us -> 65.4 us  [local(): pl.pallas_call(kernel, name='lamb', out_shape=(jax.ShapeDtypeStruct((3, R...]
    unnamed x3 -> x0, local copies, waits for them, and re-layouts: 1.84 us -> none
where the time goes in v3:
time: 69.6 us; the launch traced here: 69.1 us
  Pallas kernels  65.4 us (94%)
  local copies, waits for them, and re-layouts  3.05 us (4%)
    pallas_call x1, Pallas kernels, local(): pl.pallas_call(kernel, name='lamb', out_shape=(jax.ShapeDtypeStruct((3, R...  65.4 us
    reshape x1, local copies, waits for them, and re-layouts, local(): model.reshape(1, -1)  2.41 us

profile of v3, /device:TPU:6, one launch (start us, length us, event | category | flops | bytes accessed | tf_op | source)
XLA Modules:
  0.0 69.1 jit_solution(11265440594883495062)
XLA Ops:
  0.6 65.4 %lamb.1 = (f32[3,64,128]{2,1,0:T(8,128)S(1)}, bf16[16,4,64,128]{3,2,1,0:T(8,128)(2,1)S(1)}) custom-call(s32[40]{0:T(128)} %lengths_in.1, s32[40]{0:T(128)} %flags_in.1, f32[4096,128]{1,0:T(8,128)} %bitcast.9, f32[64,128]{1,0:T(8,128)} %bitcast.10, f32[64,128]{1,0:T(8,128)} %bitcast.11, f32[64,128]{1,0:T(8,128)} %bitcast.12), custom_call_target="tpu_custom_call" | custom-call | tf_op jit(solution)/shard_map/lamb/pallas_call | solution.py:354
  66.0 0.6 fusion
  66.7 2.4 %reshape.31 = bf16[1,524288]{1,0:T(2,128)(2,1)} reshape(bf16[524288]{0:T(1024)(128)(2,1)S(1)} %bitcast.8) | data formatting | bytes 2097152 | tf_op jit(solution)/shard_map/reshape | solution.py:390

commit v4 on v3

v4 whole, which is shorter than its diff:
```python
import jax
import jax.numpy as jnp
from jax import lax
from jax.experimental import pallas as pl
from jax.experimental.pallas import tpu as pltpu
from jax.sharding import PartitionSpec as P

MESH = pl.DeviceIdType.MESH
NZ, NX, NY, NT = 16, 4, 4, 8
ROWS = 64
WORDS = 32
NP = 40
CODED = WORDS + 1


def encode(block, unit):
    top = jnp.max(jnp.abs(block), axis=0, keepdims=True)
    scale = (top * unit).astype(jnp.int32) + 1
    inverse = (32767.0 * unit) / scale.astype(jnp.float32)
    codes = jnp.round(block * inverse).astype(jnp.int32)
    return (codes[:WORDS] << 16) + codes[WORDS:], scale


def decode(words, scale, unit):
    step = scale.astype(jnp.float32) * (1.0 / (32767.0 * unit))
    high = ((words + 32768) >> 16).astype(jnp.float32) * step
    low = ((words << 16) >> 16).astype(jnp.float32) * step
    return high, low


NEAR = (2, 14, 1, 15)
LONG = (8, 5, 11, 3, 13)
RELAYS = {3: (1,), 13: (15,), 5: (2, 1), 11: (14, 15), 8: ()}
ARRIVALS = (3, 13, 5, 11, 4, 12, 8, 6, 10, 7, 9)
FAR_FIRST = (8, 7, 9, 6, 10, 5, 11, 4, 12, 3, 13, 2, 14, 1, 15)

UNIT_X = float(2**26)
UNIT_Z = float(2**24)


def piece_sums(values, position, starts, first):
    rows = []
    for k in range(NP):
        inside = (position >= starts[k]) & (position < starts[k + 1])
        rows.append(jnp.sum(jnp.where(inside, values, 0.0), axis=0, keepdims=True))
    table = jnp.concatenate(rows, axis=0)
    totals = jnp.sum(table, axis=1, keepdims=True)
    piece = lax.broadcasted_iota(jnp.int32, (NP, 128), 0)
    lane = lax.broadcasted_iota(jnp.int32, (NP, 128), 1)
    return jnp.sum(jnp.where(piece + first == lane, totals, 0.0), axis=0, keepdims=True)


def kernel(
    lengths_in, flags_in, grads, master, avg, avg_sq,
    made, weights,
    held, coded, x_in, z_out, z_in, total, state, stat_z, stat_p, lengths, flags,
    word_sem, load_sem, state_sem, send_sem, land_sem, xr_sem, gr_sem,
):
    dp = lax.axis_index("dp")
    t = lax.axis_index("tensor")
    z, x = dp // NX, dp % NX

    def at(zz, xx, tt):
        return (zz * NX + xx, tt)

    def landed(ref, sem):
        pltpu.make_async_remote_copy(
            src_ref=ref, dst_ref=ref, send_sem=sem, recv_sem=sem,
            device_id=at(z, (x + 1) % NX, t), device_id_type=MESH,
        ).wait_recv()

    def gone(ref, sem):
        pltpu.make_async_remote_copy(
            src_ref=ref, dst_ref=ref, send_sem=sem, recv_sem=sem,
            device_id=at(z, (x + 1) % NX, t), device_id_type=MESH,
        ).wait_send()

    def load(zz):
        rows = pl.ds(pl.multiple_of(zz * (NX * ROWS), NX * ROWS), NX * ROWS)
        return pltpu.make_async_copy(grads.at[rows], held.at[rows], load_sem.at[zz])

    for o in (*FAR_FIRST, 0):
        load((z + o) % NZ).start()
    for i, ref in enumerate((master, avg, avg_sq)):
        pltpu.make_async_copy(ref, state.at[i], state_sem.at[0]).start()
    tables = [
        pltpu.make_async_copy(lengths_in, lengths, state_sem.at[1]),
        pltpu.make_async_copy(flags_in, flags, state_sem.at[2]),
    ]
    for copy in tables:
        copy.start()

    barrier = pltpu.get_barrier_semaphore()

    y, core = t // 2, t % 2

    def near(dx, dy, dc):
        return at(z, (x + dx) % NX, ((y + dy) % NY) * 2 + (core + dc) % 2)

    greeted = [near(dx, 0, 0) for dx in range(1, NX)]
    greeted += [near(0, dy, dc) for dy in range(NY) for dc in range(2) if dy or dc]
    greeted += [at((z + o) % NZ, x, t) for o in (1, 15, 2, 14, 3, 13, 4, 12)]
    for device in greeted:
        pl.semaphore_signal(barrier, 1, device_id=device, device_id_type=MESH)

    def far(i):
        return jnp.where(i % 2 == 0, NZ // 2 + i // 2, NZ // 2 - (i + 1) // 2)

    def x_copy(zz, dx):
        xx = (x + dx) % NX
        return pltpu.make_async_remote_copy(
            src_ref=coded.at[xx, zz, pl.ds(0, CODED)], dst_ref=x_in.at[x, zz, pl.ds(0, CODED)],
            send_sem=send_sem.at[0], recv_sem=xr_sem.at[zz],
            device_id=at(z, xx, t), device_id_type=MESH,
        )

    pl.semaphore_wait(barrier, len(greeted))
    for o in (4, 12):
        pl.semaphore_signal(word_sem, 1, device_id=at((z + o) % NZ, x, t), device_id_type=MESH)

    def scatter(i, c):
        zz = (z + far(i)) % NZ
        load(zz).wait()
        for dx in (2, 1, 3):
            xx = (x + dx) % NX
            start = pl.multiple_of((zz * NX + xx) * ROWS, ROWS)
            words, scale = encode(held[pl.ds(start, ROWS), :], UNIT_X)
            coded[xx, zz, :WORDS, :] = words
            coded[xx, zz, WORDS:CODED, :] = scale
            x_copy(zz, dx).start()
        return c

    lax.fori_loop(0, NZ, scatter, 0)

    for copy in tables:
        copy.wait()
    pltpu.make_async_copy(state, state, state_sem.at[0]).wait()
    starts = [jnp.int32(0)]
    split = jnp.zeros((1, 128), jnp.int32)
    lane = lax.broadcasted_iota(jnp.int32, (1, 128), 1)
    for k in range(NP):
        starts.append(starts[-1] + lengths[k])
        split = jnp.where((lane == k) | (lane == k + 64), flags[k], split)
    position = (
        dp * (ROWS * 128)
        + lax.broadcasted_iota(jnp.int32, (ROWS, 128), 0) * 128
        + lax.broadcasted_iota(jnp.int32, (ROWS, 128), 1)
    )
    w = state[0]
    w_sums = piece_sums(w * w, position, starts, 0)

    def z_copy(zz):
        return pltpu.make_async_remote_copy(
            src_ref=z_out.at[zz, pl.ds(0, CODED)], dst_ref=z_in.at[z, pl.ds(0, CODED)],
            send_sem=send_sem.at[1], recv_sem=land_sem.at[0],
            device_id=at(zz, x, t), device_id_type=MESH,
        )

    def sum_over_x(zz):
        start = pl.multiple_of((zz * NX + x) * ROWS, ROWS)
        high = held[pl.ds(start, WORDS), :]
        low = held[pl.ds(pl.multiple_of(start + WORDS, WORDS), WORDS), :]
        landed(x_in.at[pl.ds(0, NX - 1), zz, pl.ds(0, CODED)], xr_sem.at[zz])
        for dx in (1, 3, 2):
            xx = (x + dx) % NX
            h, l = decode(x_in[xx, zz, :WORDS, :], x_in[xx, zz, WORDS:CODED, :], UNIT_X)
            high, low = high + h, low + l
        return high, low

    def forward(i, c):
        zz = (z + far(i)) % NZ
        high, low = sum_over_x(zz)
        words, scale = encode(jnp.concatenate([high, low], axis=0), UNIT_Z)
        z_out[zz, :WORDS, :] = words
        z_out[zz, WORDS:CODED, :] = scale
        z_copy(zz).start()
        return c

    pl.semaphore_wait(word_sem, 2)
    lax.fori_loop(0, NZ - 1, forward, 0)
    high, low = sum_over_x(z)
    total[:WORDS, :] = high
    total[WORDS:, :] = low

    landed(z_in.at[pl.ds(0, NZ - 1), pl.ds(0, CODED)], land_sem.at[0])

    def collect(o, c):
        zz = (z + o) % NZ
        h, l = decode(z_in[zz, :WORDS, :], z_in[zz, WORDS:CODED, :], UNIT_Z)
        total[:WORDS, :] += h
        total[WORDS:, :] += l
        return c

    lax.fori_loop(1, NZ, collect, 0)

    grad = total[...] * (1.0 / (NZ * NX))
    new_avg = 0.9 * state[1] + 0.1 * grad
    new_avg_sq = 0.95 * state[2] + 0.05 * grad * grad
    made[1] = new_avg
    made[2] = new_avg_sq
    update = new_avg / (jnp.sqrt(new_avg_sq) + 1e-08) + 0.1 * state[0]
    total[...] = update
    u_sums = piece_sums(update * update, position, starts, 64)

    mine = z * 2 + core
    stat_z[mine, 0:1, :] = w_sums + u_sums
    line = [(o, dc) for o in FAR_FIRST for dc in (1, 0)] + [(0, 1)]
    for o, dc in line:
        pltpu.make_async_remote_copy(
            src_ref=stat_z.at[mine, pl.ds(0, 1)], dst_ref=stat_z.at[mine, pl.ds(0, 1)],
            send_sem=send_sem.at[2], recv_sem=land_sem.at[1],
            device_id=at((z + o) % NZ, x, y * 2 + (core + dc) % 2), device_id_type=MESH,
        ).start()
    landed(stat_z.at[pl.ds(0, len(line)), pl.ds(0, 1)], land_sem.at[1])
    own = stat_z[core, 0:1, :]
    other = stat_z[1 - core, 0:1, :]
    for zz in range(1, NZ):
        own = own + stat_z[zz * 2 + core, 0:1, :]
        other = other + stat_z[zz * 2 + 1 - core, 0:1, :]
    me = x * NY + y
    stat_p[me, 0:1, :] = own
    stat_p[me, 1:2, :] = own + other
    plane = [(dx, dy) for dx in (2, 1, 3, 0) for dy in (2, 1, 3, 0) if dx or dy]
    for dx, dy in plane:
        pltpu.make_async_remote_copy(
            src_ref=stat_p.at[me, pl.ds(0, 2)], dst_ref=stat_p.at[me, pl.ds(0, 2)],
            send_sem=send_sem.at[3], recv_sem=land_sem.at[2],
            device_id=near(dx, dy, 0), device_id_type=MESH,
        ).start()
    landed(stat_p.at[pl.ds(0, len(plane)), pl.ds(0, 2)], land_sem.at[2])
    data_sum = stat_p[y, 0:1, :]
    for xx in range(1, NX):
        data_sum = data_sum + stat_p[xx * NY + y, 0:1, :]
    tensor_sum = stat_p[0, 1:2, :]
    for i in range(1, NX * NY):
        tensor_sum = tensor_sum + stat_p[i, 1:2, :]
    effective = jnp.where(split == 1, tensor_sum, data_sum)
    norms = jnp.sqrt(effective)
    trust = norms / jnp.maximum(pltpu.roll(norms, 64, 1), 1.0)
    trust_at = jnp.broadcast_to(trust[:, 0:1], (ROWS, 128))
    for k in range(1, NP):
        trust_at = jnp.where(position >= starts[k], trust[:, k : k + 1], trust_at)
    new_weights = state[0] - 0.05 * trust_at * total[...]

    weights[z, x] = new_weights.astype(jnp.bfloat16)

    def g_copy(back, o):
        block = weights.at[(z - back) % NZ, x]
        return pltpu.make_async_remote_copy(
            src_ref=block, dst_ref=block,
            send_sem=send_sem.at[4], recv_sem=gr_sem.at[(back + o) % NZ],
            device_id=at((z + o) % NZ, x, t), device_id_type=MESH,
        )

    def f_copy(back, dx):
        block = weights.at[(z - back) % NZ, x]
        return pltpu.make_async_remote_copy(
            src_ref=block, dst_ref=block,
            send_sem=send_sem.at[5], recv_sem=land_sem.at[4 if back else 3],
            device_id=at(z, (x + dx) % NX, t), device_id_type=MESH,
        )

    def r_copy(o):
        return pltpu.make_async_remote_copy(
            src_ref=weights.at[z], dst_ref=weights.at[z],
            send_sem=send_sem.at[6], recv_sem=land_sem.at[5],
            device_id=at((z + o) % NZ, x, t), device_id_type=MESH,
        )

    def spread(back):
        for dx in (2, 1, 3):
            f_copy(back, dx).start()

    for o in LONG:
        g_copy(0, o).start()
    spread(0)
    made[0] = new_weights

    gone(coded.at[pl.ds(0, NX - 1), :, pl.ds(0, CODED)], send_sem.at[0])
    gone(z_out.at[pl.ds(0, NZ - 1), pl.ds(0, CODED)], send_sem.at[1])
    gone(stat_z.at[pl.ds(0, len(line)), pl.ds(0, 1)], send_sem.at[2])
    gone(stat_p.at[pl.ds(0, len(plane)), pl.ds(0, 2)], send_sem.at[3])

    for back in ARRIVALS:
        landed(weights.at[(z - back) % NZ, x], gr_sem.at[back])
        for o in RELAYS.get(back, ()):
            g_copy(back, o).start()
        spread(back)
        if back == 11:
            landed(weights.at[z, pl.ds(0, NX - 1)], land_sem.at[3])
            for o in NEAR:
                r_copy(o).start()
    landed(weights.at[pl.ds(0, len(ARRIVALS)), pl.ds(0, NX - 1)], land_sem.at[4])
    landed(weights.at[pl.ds(0, len(NEAR))], land_sem.at[5])

    gone(weights.at[pl.ds(0, len(ARRIVALS)), 0], send_sem.at[4])
    gone(weights.at[pl.ds(0, 1 + len(ARRIVALS)), pl.ds(0, NX - 1)], send_sem.at[5])
    gone(weights.at[pl.ds(0, len(NEAR))], send_sem.at[6])


def local(grads, piece_lengths, split_flags, master_params, exp_avg, exp_avg_sq):
    vmem = pl.BlockSpec(memory_space=pltpu.VMEM)
    anywhere = pl.BlockSpec(memory_space=pltpu.HBM)
    dma = pltpu.SemaphoreType.DMA
    hbm = lambda array: pltpu.with_memory_space_constraint(array, pltpu.HBM)
    made, model = pl.pallas_call(
        kernel,
        name="lamb",
        out_shape=(jax.ShapeDtypeStruct((3, ROWS, 128), jnp.float32), jax.ShapeDtypeStruct((NZ, NX, ROWS, 128), jnp.bfloat16)),
        in_specs=[anywhere] * 6,
        out_specs=(vmem, vmem),
        scratch_shapes=[
            pltpu.VMEM((NZ * NX * ROWS, 128), jnp.float32),
            pltpu.VMEM((NX, NZ, WORDS + 8, 128), jnp.int32),
            pltpu.VMEM((NX, NZ, WORDS + 8, 128), jnp.int32),
            pltpu.VMEM((NZ, WORDS + 8, 128), jnp.int32),
            pltpu.VMEM((NZ, WORDS + 8, 128), jnp.int32),
            pltpu.VMEM((ROWS, 128), jnp.float32),
            pltpu.VMEM((3, ROWS, 128), jnp.float32),
            pltpu.VMEM((NZ * 2, 8, 128), jnp.float32),
            pltpu.VMEM((NX * NY, 8, 128), jnp.float32),
            pltpu.SMEM((NP,), jnp.int32),
            pltpu.SMEM((NP,), jnp.int32),
            pltpu.SemaphoreType.REGULAR, dma((NZ,)), dma((3,)), dma((7,)), dma((6,)), dma((NZ,)), dma((NZ,)),
        ],
        compiler_params=pltpu.CompilerParams(
            collective_id=0, has_side_effects=True, vmem_limit_bytes=24 * 2**20
        ),
    )(
        hbm(piece_lengths), hbm(split_flags), hbm(grads.reshape(NZ * NX * ROWS, 128)),
        hbm(master_params.reshape(ROWS, 128)), hbm(exp_avg.reshape(ROWS, 128)), hbm(exp_avg_sq.reshape(ROWS, 128)),
    )
    model = lax.optimization_barrier(model.reshape(-1))
    return (
        made[0].reshape(1, -1), made[1].reshape(1, -1), made[2].reshape(1, -1), model.reshape(1, -1)
    )


def solution(mesh):
    return jax.shard_map(
        local,
        mesh=mesh,
        in_specs=(
            P("dp", "tensor", None),
            P(),
            P(),
            P("tensor", "dp"),
            P("tensor", "dp"),
            P("tensor", "dp"),
        ),
        out_specs=(P("tensor", "dp"), P("tensor", "dp"), P("tensor", "dp"), P("tensor", None)),
        check_vma=False,
    )
```

time: 69.6 us -> 63.8 us (0.917)
  Pallas kernels: 65.4 us -> 59.3 us
    pallas_call x1, Pallas kernels: 65.4 us -> 59.3 us  [local(): pl.pallas_call(kernel, name='lamb', out_shape=(jax.ShapeDtypeStruct((3, R...]
where the time goes in v4:
time: 63.8 us; the launch traced here: 63 us
  Pallas kernels  59.3 us (93%)
  local copies, waits for them, and re-layouts  3.05 us (5%)
  between operations  0.64 us (1%)
    pallas_call x1, Pallas kernels, local(): pl.pallas_call(kernel, name='lamb', out_shape=(jax.ShapeDtypeStruct((3, R...  59.3 us
    reshape x1, local copies, waits for them, and re-layouts, local(): model.reshape(1, -1)  2.41 us

profile of v4, /device:TPU:6, one launch (start us, length us, event | category | flops | bytes accessed | tf_op | source)
XLA Modules:
  0.0 63.0 jit_solution(9657663172166273190)
XLA Ops:
  0.6 59.3 %lamb.1 = (f32[3,64,128]{2,1,0:T(8,128)S(1)}, bf16[16,4,64,128]{3,2,1,0:T(8,128)(2,1)S(1)}) custom-call(s32[40]{0:T(128)} %lengths_in.1, s32[40]{0:T(128)} %flags_in.1, f32[4096,128]{1,0:T(8,128)} %bitcast.9, f32[64,128]{1,0:T(8,128)} %bitcast.10, f32[64,128]{1,0:T(8,128)} %bitcast.11, f32[64,128]{1,0:T(8,128)} %bitcast.12), custom_call_target="tpu_custom_call" | custom-call | tf_op jit(solution)/shard_map/lamb/pallas_call | solution.py:306
  59.9 0.6 %fusion = (f32[1,64,128]{2,1,0:T(8,128)}, f32[1,64,128]{2,1,0:T(8,128)}, f32[1,64,128]{2,1,0:T(8,128)}) fusion(f32[3,64,128]{2,1,0:T(8,128)S(1)} %get-tuple-element.6), kind=kLoop, calls=%fused_computation | loop fusion | bytes 196608 | tf_op jit(solution)/shard_map/slice | solution.py:335
  60.6 2.4 %reshape.31 = bf16[1,524288]{1,0:T(2,128)(2,1)} reshape(bf16[524288]{0:T(1024)(128)(2,1)S(1)} %bitcast.8) | data formatting | bytes 2097152 | tf_op jit(solution)/shard_map/reshape | solution.py:335

commit v5 on v4

--- a/solution.py
+++ b/solution.py
@@ -32,10 +32,16 @@
 LONG = (8, 5, 11, 3, 13)
 RELAYS = {3: (1,), 13: (15,), 5: (2, 1), 11: (14, 15), 8: ()}
 ARRIVALS = (3, 13, 5, 11, 4, 12, 8, 6, 10, 7, 9)
+REDUCED = (8, 7, 9, 6, 10, 4, 12, 5, 11, 3, 13)
+SENT = (8, 2, 14, 7, 1, 15, 9, 6, 10, 4, 12, 5, 11, 3, 13)
+BY_WAY = {7: (2, 0), 6: (1, 1), 9: (14, 2), 10: (15, 3), 4: (1, 4), 12: (15, 5)}
+MERGED = {5: (0, 2), 11: (2, 2), 3: (4, 1), 13: (5, 1)}
+OWN_AT = 6
+DIRECT = (8, 5, 11, 3, 13)
 FAR_FIRST = (8, 7, 9, 6, 10, 5, 11, 4, 12, 3, 13, 2, 14, 1, 15)
 
 UNIT_X = float(2**26)
-UNIT_Z = float(2**24)
+UNIT_Z = float(2**23)
 
 
 def piece_sums(values, position, starts, first):
@@ -53,8 +59,8 @@
 def kernel(
     lengths_in, flags_in, grads, master, avg, avg_sq,
     made, weights,
-    held, coded, x_in, z_out, z_in, total, state, stat_z, stat_p, lengths, flags,
-    word_sem, load_sem, state_sem, send_sem, land_sem, xr_sem, gr_sem,
+    held, coded, row_in, x_in, z_out, way_in, z_in, total, state, stat_z, stat_p, lengths, flags,
+    word_sem, load_sem, state_sem, send_sem, land_sem, xr_sem, way_sem, gr_sem,
 ):
     dp = lax.axis_index("dp")
     t = lax.axis_index("tensor")
@@ -79,7 +85,7 @@
         rows = pl.ds(pl.multiple_of(zz * (NX * ROWS), NX * ROWS), NX * ROWS)
         return pltpu.make_async_copy(grads.at[rows], held.at[rows], load_sem.at[zz])
 
-    for o in (*FAR_FIRST, 0):
+    for o in (*SENT, 0):
         load((z + o) % NZ).start()
     for i, ref in enumerate((master, avg, avg_sq)):
         pltpu.make_async_copy(ref, state.at[i], state_sem.at[0]).start()
@@ -103,9 +109,6 @@
     for device in greeted:
         pl.semaphore_signal(barrier, 1, device_id=device, device_id_type=MESH)
 
-    def far(i):
-        return jnp.where(i % 2 == 0, NZ // 2 + i // 2, NZ // 2 - (i + 1) // 2)
-
     def x_copy(zz, dx):
         xx = (x + dx) % NX
         return pltpu.make_async_remote_copy(
@@ -118,19 +121,28 @@
     for o in (4, 12):
         pl.semaphore_signal(word_sem, 1, device_id=at((z + o) % NZ, x, t), device_id_type=MESH)
 
-    def scatter(i, c):
-        zz = (z + far(i)) % NZ
+    def code(zz, xx):
+        start = pl.multiple_of((zz * NX + xx) * ROWS, ROWS)
+        words, scale = encode(held[pl.ds(start, ROWS), :], UNIT_X)
+        coded[xx, zz, :WORDS, :] = words
+        coded[xx, zz, WORDS:CODED, :] = scale
+
+    for o in SENT:
+        zz = (z + o) % NZ
         load(zz).wait()
-        for dx in (2, 1, 3):
-            xx = (x + dx) % NX
-            start = pl.multiple_of((zz * NX + xx) * ROWS, ROWS)
-            words, scale = encode(held[pl.ds(start, ROWS), :], UNIT_X)
-            coded[xx, zz, :WORDS, :] = words
-            coded[xx, zz, WORDS:CODED, :] = scale
-            x_copy(zz, dx).start()
-        return c
-
-    lax.fori_loop(0, NZ, scatter, 0)
+        if o in NEAR:
+            for xx in range(NX):
+                code(zz, xx)
+            pltpu.make_async_remote_copy(
+                src_ref=coded.at[:, zz, pl.ds(0, CODED)],
+                dst_ref=row_in.at[NEAR.index(o), :, pl.ds(0, CODED)],
+                send_sem=send_sem.at[7], recv_sem=land_sem.at[6],
+                device_id=at(zz, x, t), device_id_type=MESH,
+            ).start()
+        else:
+            for dx in (2, 1, 3):
+                code(zz, (x + dx) % NX)
+                x_copy(zz, dx).start()
 
     for copy in tables:
         copy.wait()
@@ -149,49 +161,68 @@
     w = state[0]
     w_sums = piece_sums(w * w, position, starts, 0)
 
-    def z_copy(zz):
-        return pltpu.make_async_remote_copy(
-            src_ref=z_out.at[zz, pl.ds(0, CODED)], dst_ref=z_in.at[z, pl.ds(0, CODED)],
-            send_sem=send_sem.at[1], recv_sem=land_sem.at[0],
-            device_id=at(zz, x, t), device_id_type=MESH,
-        )
-
-    def sum_over_x(zz):
-        start = pl.multiple_of((zz * NX + x) * ROWS, ROWS)
-        high = held[pl.ds(start, WORDS), :]
-        low = held[pl.ds(pl.multiple_of(start + WORDS, WORDS), WORDS), :]
+    def sum_over_x(zz, high, low, unit):
         landed(x_in.at[pl.ds(0, NX - 1), zz, pl.ds(0, CODED)], xr_sem.at[zz])
         for dx in (1, 3, 2):
             xx = (x + dx) % NX
-            h, l = decode(x_in[xx, zz, :WORDS, :], x_in[xx, zz, WORDS:CODED, :], UNIT_X)
+            h, l = decode(x_in[xx, zz, :WORDS, :], x_in[xx, zz, WORDS:CODED, :], unit)
             high, low = high + h, low + l
         return high, low
 
-    def forward(i, c):
-        zz = (z + far(i)) % NZ
-        high, low = sum_over_x(zz)
+    def halves(zz, xx):
+        start = pl.multiple_of((zz * NX + xx) * ROWS, ROWS)
+        return held[pl.ds(start, WORDS), :], held[pl.ds(pl.multiple_of(start + WORDS, WORDS), WORDS), :]
+
+    def sum_over_near(xx):
+        high, low = halves(z, xx)
+        for n in range(len(NEAR)):
+            h, l = decode(row_in[n, xx, :WORDS, :], row_in[n, xx, WORDS:CODED, :], UNIT_X)
+            high, low = high + h, low + l
+        return high, low
+
+    pl.semaphore_wait(word_sem, 2)
+    for n, o in enumerate(REDUCED):
+        if n == OWN_AT:
+            load(z).wait()
+            landed(row_in.at[:, :, pl.ds(0, CODED)], land_sem.at[6])
+            for dx in (2, 1, 3):
+                xx = (x + dx) % NX
+                words, scale = encode(jnp.concatenate(sum_over_near(xx), axis=0), UNIT_Z)
+                coded[xx, z, :WORDS, :] = words
+                coded[xx, z, WORDS:CODED, :] = scale
+                x_copy(z, dx).start()
+            high, low = sum_over_near(x)
+            total[:WORDS, :] = high
+            total[WORDS:, :] = low
+        zz = (z + o) % NZ
+        high, low = sum_over_x(zz, *halves(zz, x), UNIT_X)
+        if o in MERGED:
+            first, count = MERGED[o]
+            landed(way_in.at[pl.ds(first, count), pl.ds(0, CODED)], way_sem.at[first])
+            for slot in range(first, first + count):
+                h, l = decode(way_in[slot, :WORDS, :], way_in[slot, WORDS:CODED, :], UNIT_Z)
+                high, low = high + h, low + l
         words, scale = encode(jnp.concatenate([high, low], axis=0), UNIT_Z)
-        z_out[zz, :WORDS, :] = words
-        z_out[zz, WORDS:CODED, :] = scale
-        z_copy(zz).start()
-        return c
-
-    pl.semaphore_wait(word_sem, 2)
-    lax.fori_loop(0, NZ - 1, forward, 0)
-    high, low = sum_over_x(z)
+        z_out[n, :WORDS, :] = words
+        z_out[n, WORDS:CODED, :] = scale
+        if o in BY_WAY:
+            to, slot = BY_WAY[o]
+            target, sem = way_in.at[slot], way_sem.at[0 if slot < 2 else 2 if slot < 4 else slot]
+        else:
+            to = o
+            target, sem = z_in.at[DIRECT.index(o)], land_sem.at[0]
+        pltpu.make_async_remote_copy(
+            src_ref=z_out.at[n, pl.ds(0, CODED)], dst_ref=target.at[pl.ds(0, CODED)],
+            send_sem=send_sem.at[1], recv_sem=sem,
+            device_id=at((z + to) % NZ, x, t), device_id_type=MESH,
+        ).start()
+    high, low = sum_over_x(z, total[:WORDS, :], total[WORDS:, :], UNIT_Z)
+    landed(z_in.at[pl.ds(0, len(DIRECT)), pl.ds(0, CODED)], land_sem.at[0])
+    for n in range(len(DIRECT)):
+        h, l = decode(z_in[n, :WORDS, :], z_in[n, WORDS:CODED, :], UNIT_Z)
+        high, low = high + h, low + l
     total[:WORDS, :] = high
     total[WORDS:, :] = low
-
-    landed(z_in.at[pl.ds(0, NZ - 1), pl.ds(0, CODED)], land_sem.at[0])
-
-    def collect(o, c):
-        zz = (z + o) % NZ
-        h, l = decode(z_in[zz, :WORDS, :], z_in[zz, WORDS:CODED, :], UNIT_Z)
-        total[:WORDS, :] += h
-        total[WORDS:, :] += l
-        return c
-
-    lax.fori_loop(1, NZ, collect, 0)
 
     grad = total[...] * (1.0 / (NZ * NX))
     new_avg = 0.9 * state[1] + 0.1 * grad
@@ -276,8 +307,9 @@
     spread(0)
     made[0] = new_weights
 
-    gone(coded.at[pl.ds(0, NX - 1), :, pl.ds(0, CODED)], send_sem.at[0])
-    gone(z_out.at[pl.ds(0, NZ - 1), pl.ds(0, CODED)], send_sem.at[1])
+    gone(coded.at[pl.ds(0, NX - 1), pl.ds(0, len(REDUCED) + 1), pl.ds(0, CODED)], send_sem.at[0])
+    gone(coded.at[:, pl.ds(0, len(NEAR)), pl.ds(0, CODED)], send_sem.at[7])
+    gone(z_out.at[pl.ds(0, len(REDUCED)), pl.ds(0, CODED)], send_sem.at[1])
     gone(stat_z.at[pl.ds(0, len(line)), pl.ds(0, 1)], send_sem.at[2])
     gone(stat_p.at[pl.ds(0, len(plane)), pl.ds(0, 2)], send_sem.at[3])
 
@@ -312,16 +344,18 @@
         scratch_shapes=[
             pltpu.VMEM((NZ * NX * ROWS, 128), jnp.float32),
             pltpu.VMEM((NX, NZ, WORDS + 8, 128), jnp.int32),
+            pltpu.VMEM((len(NEAR), NX, WORDS + 8, 128), jnp.int32),
             pltpu.VMEM((NX, NZ, WORDS + 8, 128), jnp.int32),
             pltpu.VMEM((NZ, WORDS + 8, 128), jnp.int32),
-            pltpu.VMEM((NZ, WORDS + 8, 128), jnp.int32),
+            pltpu.VMEM((len(BY_WAY), WORDS + 8, 128), jnp.int32),
+            pltpu.VMEM((len(DIRECT), WORDS + 8, 128), jnp.int32),
             pltpu.VMEM((ROWS, 128), jnp.float32),
             pltpu.VMEM((3, ROWS, 128), jnp.float32),
             pltpu.VMEM((NZ * 2, 8, 128), jnp.float32),
             pltpu.VMEM((NX * NY, 8, 128), jnp.float32),
             pltpu.SMEM((NP,), jnp.int32),
             pltpu.SMEM((NP,), jnp.int32),
-            pltpu.SemaphoreType.REGULAR, dma((NZ,)), dma((3,)), dma((7,)), dma((6,)), dma((NZ,)), dma((NZ,)),
+            pltpu.SemaphoreType.REGULAR, dma((NZ,)), dma((3,)), dma((8,)), dma((7,)), dma((NZ,)), dma((6,)), dma((NZ,)),
         ],
         compiler_params=pltpu.CompilerParams(
             collective_id=0, has_side_effects=True, vmem_limit_bytes=24 * 2**20

time: 63.8 us -> 63.5 us (level)
  the two profiles are of different devices: /device:TPU:6 before, /device:TPU:2 now
where the time goes in v5:
time: 63.5 us; the launch traced here: 63.4 us
  Pallas kernels  59.7 us (94%)
  local copies, waits for them, and re-layouts  3.05 us (5%)
  between operations  0.64 us (1%)
    pallas_call x1, Pallas kernels, local(): pl.pallas_call(kernel, name='lamb', out_shape=(jax.ShapeDtypeStruct((3, R...  59.7 us
    reshape x1, local copies, waits for them, and re-layouts, local(): model.reshape(1, -1)  2.41 us

profile of v5, /device:TPU:2, one launch (start us, length us, event | category | flops | bytes accessed | tf_op | source)
XLA Modules:
  0.0 63.4 jit_solution(16770963412093115116)
XLA Ops:
  0.6 59.7 %lamb.1 = (f32[3,64,128]{2,1,0:T(8,128)S(1)}, bf16[16,4,64,128]{3,2,1,0:T(8,128)(2,1)S(1)}) custom-call(s32[40]{0:T(128)} %lengths_in.1, s32[40]{0:T(128)} %flags_in.1, f32[4096,128]{1,0:T(8,128)} %bitcast.9, f32[64,128]{1,0:T(8,128)} %bitcast.10, f32[64,128]{1,0:T(8,128)} %bitcast.11, f32[64,128]{1,0:T(8,128)} %bitcast.12), custom_call_target="tpu_custom_call" | custom-call | tf_op jit(solution)/shard_map/lamb/pallas_call | solution.py:338
  60.4 0.6 %fusion = (f32[1,64,128]{2,1,0:T(8,128)}, f32[1,64,128]{2,1,0:T(8,128)}, f32[1,64,128]{2,1,0:T(8,128)}) fusion(f32[3,64,128]{2,1,0:T(8,128)S(1)} %get-tuple-element.6), kind=kLoop, calls=%fused_computation | loop fusion | bytes 196608 | tf_op jit(solution)/shard_map/slice | solution.py:369
  61.0 2.4 %reshape.31 = bf16[1,524288]{1,0:T(2,128)(2,1)} reshape(bf16[524288]{0:T(1024)(128)(2,1)S(1)} %bitcast.8) | data formatting | bytes 2097152 | tf_op jit(solution)/shard_map/reshape | solution.py:369

commit v6 on v5

--- a/solution.py
+++ b/solution.py
@@ -58,8 +58,8 @@
 
 def kernel(
     lengths_in, flags_in, grads, master, avg, avg_sq,
-    made, weights,
-    held, coded, row_in, x_in, z_out, way_in, z_in, total, state, stat_z, stat_p, lengths, flags,
+    made, model,
+    weights, held, coded, row_in, x_in, z_out, way_in, z_in, total, state, stat_z, stat_p, lengths, flags,
     word_sem, load_sem, state_sem, send_sem, land_sem, xr_sem, way_sem, gr_sem,
 ):
     dp = lax.axis_index("dp")
@@ -287,14 +287,14 @@
         block = weights.at[(z - back) % NZ, x]
         return pltpu.make_async_remote_copy(
             src_ref=block, dst_ref=block,
-            send_sem=send_sem.at[5], recv_sem=land_sem.at[4 if back else 3],
+            send_sem=send_sem.at[5], recv_sem=xr_sem.at[back],
             device_id=at(z, (x + dx) % NX, t), device_id_type=MESH,
         )
 
     def r_copy(o):
         return pltpu.make_async_remote_copy(
             src_ref=weights.at[z], dst_ref=weights.at[z],
-            send_sem=send_sem.at[6], recv_sem=land_sem.at[5],
+            send_sem=send_sem.at[6], recv_sem=way_sem.at[NEAR.index(o)],
             device_id=at((z + o) % NZ, x, t), device_id_type=MESH,
         )
 
@@ -319,11 +319,23 @@
             g_copy(back, o).start()
         spread(back)
         if back == 11:
-            landed(weights.at[z, pl.ds(0, NX - 1)], land_sem.at[3])
+            landed(weights.at[z, pl.ds(0, NX - 1)], xr_sem.at[0])
             for o in NEAR:
                 r_copy(o).start()
-    landed(weights.at[pl.ds(0, len(ARRIVALS)), pl.ds(0, NX - 1)], land_sem.at[4])
-    landed(weights.at[pl.ds(0, len(NEAR))], land_sem.at[5])
+
+    for back in (0, 3, 13, 5, 11, 1, 15, 4, 12, 2, 14, 8, 6, 10, 7, 9):
+        zz = (z - back) % NZ
+        if back in NEAR:
+            landed(weights.at[zz], way_sem.at[NEAR.index(back)])
+        elif back:
+            landed(weights.at[zz, pl.ds(0, NX - 1)], xr_sem.at[back])
+
+        def place(xx, c, zz=zz):
+            start = pl.multiple_of((zz * NX + xx) * ROWS, ROWS)
+            model[pl.ds(start, ROWS), :, :] = weights[zz, xx][:, None, :]
+            return c
+
+        lax.fori_loop(0, NX, place, 0)
 
     gone(weights.at[pl.ds(0, len(ARRIVALS)), 0], send_sem.at[4])
     gone(weights.at[pl.ds(0, 1 + len(ARRIVALS)), pl.ds(0, NX - 1)], send_sem.at[5])
@@ -338,10 +350,11 @@
     made, model = pl.pallas_call(
         kernel,
         name="lamb",
-        out_shape=(jax.ShapeDtypeStruct((3, ROWS, 128), jnp.float32), jax.ShapeDtypeStruct((NZ, NX, ROWS, 128), jnp.bfloat16)),
+        out_shape=(jax.ShapeDtypeStruct((3, ROWS, 128), jnp.float32), jax.ShapeDtypeStruct((NZ * NX * ROWS, 1, 128), jnp.bfloat16)),
         in_specs=[anywhere] * 6,
         out_specs=(vmem, vmem),
         scratch_shapes=[
+            pltpu.VMEM((NZ, NX, ROWS, 128), jnp.bfloat16),
             pltpu.VMEM((NZ * NX * ROWS, 128), jnp.float32),
             pltpu.VMEM((NX, NZ, WORDS + 8, 128), jnp.int32),
             pltpu.VMEM((len(NEAR), NX, WORDS + 8, 128), jnp.int32),
@@ -364,7 +377,6 @@
         hbm(piece_lengths), hbm(split_flags), hbm(grads.reshape(NZ * NX * ROWS, 128)),
         hbm(master_params.reshape(ROWS, 128)), hbm(exp_avg.reshape(ROWS, 128)), hbm(exp_avg_sq.reshape(ROWS, 128)),
     )
-    model = lax.optimization_barrier(model.reshape(-1))
     return (
         made[0].reshape(1, -1), made[1].reshape(1, -1), made[2].reshape(1, -1), model.reshape(1, -1)
     )

time: 63.5 us -> 62.6 us (0.986)
  local copies, waits for them, and re-layouts: 3.05 us -> 1.96 us
    reshape x1 -> x0, local copies, waits for them, and re-layouts: 2.41 us -> none  [local(): model.reshape(1, -1)]
    unnamed x0 -> x1, local copies, waits for them, and re-layouts: none -> 1.32 us
where the time goes in v6:
time: 62.6 us; the launch traced here: 62.4 us
  Pallas kernels  59.8 us (96%)
  local copies, waits for them, and re-layouts  1.96 us (3%)
  between operations  0.64 us (1%)
    pallas_call x1, Pallas kernels, local(): pl.pallas_call(kernel, name='lamb', out_shape=(jax.ShapeDtypeStruct((3, R...  59.8 us
    unnamed x1, local copies, waits for them, and re-layouts  1.32 us

profile of v6, /device:TPU:2, one launch (start us, length us, event | category | flops | bytes accessed | tf_op | source)
XLA Modules:
  0.0 62.4 jit_solution(11502161096678135348)
XLA Ops:
  0.6 59.8 %lamb.1 = (f32[3,64,128]{2,1,0:T(8,128)S(1)}, bf16[4096,1,128]{2,1,0:T(2,128)(2,1)S(1)}) custom-call(s32[40]{0:T(128)} %lengths_in.1, s32[40]{0:T(128)} %flags_in.1, f32[4096,128]{1,0:T(8,128)} %bitcast.9, f32[64,128]{1,0:T(8,128)} %bitcast.10, f32[64,128]{1,0:T(8,128)} %bitcast.11, f32[64,128]{1,0:T(8,128)} %bitcast.12), custom_call_target="tpu_custom_call" | custom-call | tf_op jit(solution)/shard_map/lamb/pallas_call | solution.py:350
  60.5 0.6 %fusion = (f32[1,64,128]{2,1,0:T(8,128)}, f32[1,64,128]{2,1,0:T(8,128)}, f32[1,64,128]{2,1,0:T(8,128)}) fusion(f32[3,64,128]{2,1,0:T(8,128)S(1)} %get-tuple-element.6), kind=kLoop, calls=%fused_computation | loop fusion | bytes 196608 | tf_op jit(solution)/shard_map/slice | solution.py:381
  61.1 1.3 %copy.11 = bf16[1,524288]{1,0:T(2,128)(2,1)} copy(bf16[1,524288]{1,0:T(2,128)(2,1)S(1)} %bitcast.8) | data formatting | bytes 2097152

commit v7 on v6

--- a/solution.py
+++ b/solution.py
@@ -60,7 +60,7 @@
     lengths_in, flags_in, grads, master, avg, avg_sq,
     made, model,
     weights, held, coded, row_in, x_in, z_out, way_in, z_in, total, state, stat_z, stat_p, lengths, flags,
-    word_sem, load_sem, state_sem, send_sem, land_sem, xr_sem, way_sem, gr_sem,
+    word_sem, load_sem, state_sem, send_sem, land_sem, xr_sem, way_sem,
 ):
     dp = lax.axis_index("dp")
     t = lax.axis_index("tensor")
@@ -81,33 +81,25 @@
             device_id=at(z, (x + 1) % NX, t), device_id_type=MESH,
         ).wait_send()
 
+    barrier = pltpu.get_barrier_semaphore()
+
+    y, core = t // 2, t % 2
+
+    def near(dx, dy, dc):
+        return at(z, (x + dx) % NX, ((y + dy) % NY) * 2 + (core + dc) % 2)
+
+    greeted = [at((z + o) % NZ, x, t) for o in (4, 12, 3, 13, 2, 14, 1, 15)]
+    greeted += [near(dx, 0, 0) for dx in range(1, NX)]
+    greeted += [near(0, dy, dc) for dy in range(NY) for dc in range(2) if dy or dc]
+    for device in greeted:
+        pl.semaphore_signal(barrier, 1, device_id=device, device_id_type=MESH)
+
     def load(zz):
         rows = pl.ds(pl.multiple_of(zz * (NX * ROWS), NX * ROWS), NX * ROWS)
         return pltpu.make_async_copy(grads.at[rows], held.at[rows], load_sem.at[zz])
 
     for o in (*SENT, 0):
         load((z + o) % NZ).start()
-    for i, ref in enumerate((master, avg, avg_sq)):
-        pltpu.make_async_copy(ref, state.at[i], state_sem.at[0]).start()
-    tables = [
-        pltpu.make_async_copy(lengths_in, lengths, state_sem.at[1]),
-        pltpu.make_async_copy(flags_in, flags, state_sem.at[2]),
-    ]
-    for copy in tables:
-        copy.start()
-
-    barrier = pltpu.get_barrier_semaphore()
-
-    y, core = t // 2, t % 2
-
-    def near(dx, dy, dc):
-        return at(z, (x + dx) % NX, ((y + dy) % NY) * 2 + (core + dc) % 2)
-
-    greeted = [near(dx, 0, 0) for dx in range(1, NX)]
-    greeted += [near(0, dy, dc) for dy in range(NY) for dc in range(2) if dy or dc]
-    greeted += [at((z + o) % NZ, x, t) for o in (1, 15, 2, 14, 3, 13, 4, 12)]
-    for device in greeted:
-        pl.semaphore_signal(barrier, 1, device_id=device, device_id_type=MESH)
 
     def x_copy(zz, dx):
         xx = (x + dx) % NX
@@ -127,7 +119,16 @@
         coded[xx, zz, :WORDS, :] = words
         coded[xx, zz, WORDS:CODED, :] = scale
 
-    for o in SENT:
+    tables = [
+        pltpu.make_async_copy(lengths_in, lengths, state_sem.at[1]),
+        pltpu.make_async_copy(flags_in, flags, state_sem.at[2]),
+    ]
+    for n, o in enumerate(SENT):
+        if n == 3:
+            for i, ref in enumerate((master, avg, avg_sq)):
+                pltpu.make_async_copy(ref, state.at[i], state_sem.at[0]).start()
+            for copy in tables:
+                copy.start()
         zz = (z + o) % NZ
         load(zz).wait()
         if o in NEAR:
@@ -136,7 +137,7 @@
             pltpu.make_async_remote_copy(
                 src_ref=coded.at[:, zz, pl.ds(0, CODED)],
                 dst_ref=row_in.at[NEAR.index(o), :, pl.ds(0, CODED)],
-                send_sem=send_sem.at[7], recv_sem=land_sem.at[6],
+                send_sem=send_sem.at[7], recv_sem=land_sem.at[3],
                 device_id=at(zz, x, t), device_id_type=MESH,
             ).start()
         else:
@@ -184,7 +185,7 @@
     for n, o in enumerate(REDUCED):
         if n == OWN_AT:
             load(z).wait()
-            landed(row_in.at[:, :, pl.ds(0, CODED)], land_sem.at[6])
+            landed(row_in.at[:, :, pl.ds(0, CODED)], land_sem.at[3])
             for dx in (2, 1, 3):
                 xx = (x + dx) % NX
                 words, scale = encode(jnp.concatenate(sum_over_near(xx), axis=0), UNIT_Z)
@@ -279,7 +280,7 @@
         block = weights.at[(z - back) % NZ, x]
         return pltpu.make_async_remote_copy(
             src_ref=block, dst_ref=block,
-            send_sem=send_sem.at[4], recv_sem=gr_sem.at[(back + o) % NZ],
+            send_sem=send_sem.at[4], recv_sem=load_sem.at[(back + o) % NZ],
             device_id=at((z + o) % NZ, x, t), device_id_type=MESH,
         )
 
@@ -314,7 +315,7 @@
     gone(stat_p.at[pl.ds(0, len(plane)), pl.ds(0, 2)], send_sem.at[3])
 
     for back in ARRIVALS:
-        landed(weights.at[(z - back) % NZ, x], gr_sem.at[back])
+        landed(weights.at[(z - back) % NZ, x], load_sem.at[back])
         for o in RELAYS.get(back, ()):
             g_copy(back, o).start()
         spread(back)
@@ -368,7 +369,7 @@
             pltpu.VMEM((NX * NY, 8, 128), jnp.float32),
             pltpu.SMEM((NP,), jnp.int32),
             pltpu.SMEM((NP,), jnp.int32),
-            pltpu.SemaphoreType.REGULAR, dma((NZ,)), dma((3,)), dma((8,)), dma((7,)), dma((NZ,)), dma((6,)), dma((NZ,)),
+            pltpu.SemaphoreType.REGULAR, dma((NZ,)), dma((3,)), dma((8,)), dma((4,)), dma((NZ,)), dma((6,)),
         ],
         compiler_params=pltpu.CompilerParams(
             collective_id=0, has_side_effects=True, vmem_limit_bytes=24 * 2**20

time: 62.6 us -> 62.2 us (level)
  no operation moved by 1% of the time
where the time goes in v7:
time: 62.2 us; the launch traced here: 62.1 us
  Pallas kernels  59.5 us (96%)
  local copies, waits for them, and re-layouts  1.96 us (3%)
  between operations  0.64 us (1%)
    pallas_call x1, Pallas kernels, local(): pl.pallas_call(kernel, name='lamb', out_shape=(jax.ShapeDtypeStruct((3, R...  59.5 us
    unnamed x1, local copies, waits for them, and re-layouts  1.32 us

profile of v7, /device:TPU:2, one launch (start us, length us, event | category | flops | bytes accessed | tf_op | source)
XLA Modules:
  0.0 62.1 jit_solution(18413562025599822021)
XLA Ops:
  0.6 59.5 %lamb.1 = (f32[3,64,128]{2,1,0:T(8,128)S(1)}, bf16[4096,1,128]{2,1,0:T(2,128)(2,1)S(1)}) custom-call(s32[40]{0:T(128)} %lengths_in.1, s32[40]{0:T(128)} %flags_in.1, f32[4096,128]{1,0:T(8,128)} %bitcast.9, f32[64,128]{1,0:T(8,128)} %bitcast.10, f32[64,128]{1,0:T(8,128)} %bitcast.11, f32[64,128]{1,0:T(8,128)} %bitcast.12), custom_call_target="tpu_custom_call" | custom-call | tf_op jit(solution)/shard_map/lamb/pallas_call | solution.py:351
  60.1 0.6 %fusion = (f32[1,64,128]{2,1,0:T(8,128)}, f32[1,64,128]{2,1,0:T(8,128)}, f32[1,64,128]{2,1,0:T(8,128)}) fusion(f32[3,64,128]{2,1,0:T(8,128)S(1)} %get-tuple-element.6), kind=kLoop, calls=%fused_computation | loop fusion | bytes 196608 | tf_op jit(solution)/shard_map/slice | solution.py:382
  60.7 1.3 %copy.11 = bf16[1,524288]{1,0:T(2,128)(2,1)} copy(bf16[1,524288]{1,0:T(2,128)(2,1)S(1)} %bitcast.8) | data formatting | bytes 2097152

commit v8 on v7

--- a/solution.py
+++ b/solution.py
@@ -36,7 +36,7 @@
 SENT = (8, 2, 14, 7, 1, 15, 9, 6, 10, 4, 12, 5, 11, 3, 13)
 BY_WAY = {7: (2, 0), 6: (1, 1), 9: (14, 2), 10: (15, 3), 4: (1, 4), 12: (15, 5)}
 MERGED = {5: (0, 2), 11: (2, 2), 3: (4, 1), 13: (5, 1)}
-OWN_AT = 6
+OWN_AT = 8
 DIRECT = (8, 5, 11, 3, 13)
 FAR_FIRST = (8, 7, 9, 6, 10, 5, 11, 4, 12, 3, 13, 2, 14, 1, 15)
 

time: 62.2 us -> 62 us (level)
  the two profiles are of different devices: /device:TPU:2 before, /device:TPU:6 now
where the time goes in v8:
time: 62 us; the launch traced here: 61.9 us
  Pallas kernels  59.3 us (96%)
  local copies, waits for them, and re-layouts  1.96 us (3%)
  between operations  0.64 us (1%)
    pallas_call x1, Pallas kernels, local(): pl.pallas_call(kernel, name='lamb', out_shape=(jax.ShapeDtypeStruct((3, R...  59.3 us
    unnamed x1, local copies, waits for them, and re-layouts  1.32 us

profile of v8, /device:TPU:6, one launch (start us, length us, event | category | flops | bytes accessed | tf_op | source)
XLA Modules:
  0.0 61.9 jit_solution(2041399465388405381)
XLA Ops:
  0.6 59.3 %lamb.1 = (f32[3,64,128]{2,1,0:T(8,128)S(1)}, bf16[4096,1,128]{2,1,0:T(2,128)(2,1)S(1)}) custom-call(s32[40]{0:T(128)} %lengths_in.1, s32[40]{0:T(128)} %flags_in.1, f32[4096,128]{1,0:T(8,128)} %bitcast.9, f32[64,128]{1,0:T(8,128)} %bitcast.10, f32[64,128]{1,0:T(8,128)} %bitcast.11, f32[64,128]{1,0:T(8,128)} %bitcast.12), custom_call_target="tpu_custom_call" | custom-call | tf_op jit(solution)/shard_map/lamb/pallas_call | solution.py:351
  60.0 0.6 %fusion = (f32[1,64,128]{2,1,0:T(8,128)}, f32[1,64,128]{2,1,0:T(8,128)}, f32[1,64,128]{2,1,0:T(8,128)}) fusion(f32[3,64,128]{2,1,0:T(8,128)S(1)} %get-tuple-element.6), kind=kLoop, calls=%fused_computation | loop fusion | bytes 196608 | tf_op jit(solution)/shard_map/slice | solution.py:382
  60.6 1.3 %copy.11 = bf16[1,524288]{1,0:T(2,128)(2,1)} copy(bf16[1,524288]{1,0:T(2,128)(2,1)S(1)} %bitcast.8) | data formatting | bytes 2097152
